TPU v7x, 256 devices: a whole 4x4x8 slice. The times are simulated.
256 devices in a mesh: replica: 16 (over z, x_hi), shard: 16 (over y, x_lo, core).
Axes of the slice: x: 4 (x_hi: 2, x_lo: 2; x = x_hi * 2 + x_lo), y: 4, z: 8, core: 2. Of those that a mesh axis runs over, the one named last changes fastest.
Arguments:
- params: float32 [16, 4096, 1024], P('replica', 'shard'), may hold values from -0.09375 to 0.09375
- first_moment: float32 [16, 4096, 1024], P('replica', 'shard'), may hold values from -6 to 6
- second_moment: float32 [16, 4096, 1024], P('replica', 'shard'), may hold values from 0.02 to 0.5
- push_weight: float32 [16], P('replica'), may hold values from 0.5 to 2
- tokens: bfloat16 [16, 8192, 4096], P('replica', 'shard'), may hold values from -6 to 6
- cotangent: bfloat16 [16, 8192, 1024], P('replica', 'shard'), may hold values from -0.1796875 to 0.1796875
- gossip_round: int32 [1], replicated, may hold values from 0 to 15
Outputs:
- new_params: float32 [16, 4096, 1024], P('replica', 'shard')
- new_first: float32 [16, 4096, 1024], P('replica', 'shard')
- new_second: float32 [16, 4096, 1024], P('replica', 'shard')
- new_weight: float32 [16], P('replica')
- activation: bfloat16 [16, 8192, 1024], P('replica', 'shard')
All inputs are finite; a program needn't handle non-finite values.
Results may differ from a plain program's by a relative error of at most 0.009.
Values may be sent and summed in bfloat16 or wider, within the bound.
A program may use at most 128 MiB of HBM per device.

v0:
```python
from functools import partial

import jax
import jax.numpy as jnp
from jax import lax
from jax.sharding import PartitionSpec as P

STEP_COUNT = 20


beta_one = 0.9
beta_two = 0.999
rate = 0.003
epsilon = 1e-08


def shortened(value):

    def short(part):
        return part.astype(jnp.bfloat16) if part.dtype == jnp.float32 else part

    return jax.tree.map(short, value)


def passed_along(block, axis, distance):
    devices = range(lax.axis_size(axis))
    route = [((i - distance) % len(devices), i) for i in devices]
    return lax.ppermute(block, axis, route)


def adam_update(param_block, first_block, second_block, gradient):
    correct_one = 1.0 - beta_one ** (STEP_COUNT + 1)
    correct_two = 1.0 - beta_two ** (STEP_COUNT + 1)
    fresh_first = beta_one * first_block + (1.0 - beta_one) * gradient
    fresh_second = beta_two * second_block + (1.0 - beta_two) * (gradient * gradient)
    update = fresh_first / correct_one / (jnp.sqrt(fresh_second / correct_two) + epsilon)
    return (param_block - rate * update, fresh_first, fresh_second)


def push_new(values, offset):
    return jax.tree.map(
        lambda part, own: part.astype(own.dtype),
        passed_along(shortened(values), "replica", offset),
        values,
    )


def by_level(sender, values, level_index, levels):
    branches = [partial(sender, offset=1 << exponent) for exponent in range(levels)]
    return lax.switch(level_index, branches, values)


def per_device(params, first_moment, second_moment, push_weight, tokens, cotangent, gossip_round):
    param_shard = params[0]
    first_shard = first_moment[0]
    second_shard = second_moment[0]
    token_rows = tokens[0]
    cotangent_rows = cotangent[0]
    levels = lax.axis_size("replica").bit_length() - 1
    level_index = gossip_round[0] % levels
    weight = (param_shard / push_weight[0]).astype(jnp.bfloat16)
    columns = token_rows
    summed = jnp.dot(
        columns,
        lax.all_gather(weight, "shard", axis=0, tiled=True),
        preferred_element_type=jnp.float32,
    )
    activation = summed.astype(jnp.bfloat16)
    columns = token_rows
    gradient = lax.psum_scatter(
        lax.dot_general(
            columns, cotangent_rows, (((0,), (0,)), ((), ())), preferred_element_type=jnp.float32
        ).astype(jnp.bfloat16),
        "shard",
        scatter_dimension=0,
        tiled=True,
    ).astype(jnp.float32)
    stepped = adam_update(param_shard, first_shard, second_shard, gradient)
    peer_all = by_level(
        push_new, (stepped[0], stepped[1], stepped[2], push_weight), level_index, levels
    )
    theirs = (peer_all[0], peer_all[1], peer_all[2])
    peer_scale = peer_all[3]
    new_params = 0.5 * (stepped[0] + theirs[0])
    new_first = 0.5 * (stepped[1] + theirs[1])
    new_second = 0.5 * (stepped[2] + theirs[2])
    new_weight = 0.5 * (push_weight + peer_scale)
    return (new_params[None], new_first[None], new_second[None], new_weight, activation[None])


def solution(mesh):
    placed = (
        P("replica", "shard", None),
        P("replica", "shard", None),
        P("replica", "shard", None),
        P("replica"),
        P("replica", "shard", None),
        P("replica", "shard", None),
        P(),
    )
    return jax.shard_map(
        per_device,
        mesh=mesh,
        in_specs=placed,
        out_specs=(
            P("replica", "shard", None),
            P("replica", "shard", None),
            P("replica", "shard", None),
            P("replica"),
            P("replica", "shard", None),
        ),
        check_vma=False,
    )
```

profile of v0, /device:TPU:32, one launch (start us, length us, event | category | flops | bytes accessed | tf_op | source)
XLA Modules:
  0.0 224.4 jit_solution(503993070915904201)
XLA Ops:
  7.2 0.0 copy-start
  7.2 0.0 reduce-scatter.2.cloned.1.call-start
  7.2 1.2 copy-done
  8.4 9.1 %convolution_convert_fusion = bf16[4096,1024]{1,0:T(8,128)(2,1)} fusion(bf16[1,512,4096]{2,1,0:T(8,128)(2,1)} %param.15, bf16[1,512,1024]{2,1,0:T(8,128)(2,1)S(1)} %copy-done), kind=kOutput, calls=%fused_computation | convolution fusion | flops 4299161600 | bytes 13631488 | tf_op jit(solution)/shard_map/dot_general | solution.py:71
  17.4 0.0 reduce-scatter.2.cloned.1.call-update
  17.5 0.0 all-gather.2.cloned.1.call-start
  18.2 102.4 %reduce-scatter.2.cloned.1.call-done = bf16[256,1024]{1,0:T(8,128)(2,1)} async-done(((bf16[4096,1024]{1,0:T(8,128)(2,1)}), bf16[256,1024]{1,0:T(8,128)(2,1)}) %reduce-scatter.2.cloned.1.call-update) | async-done | bytes 524304 | tf_op jit(solution)/shard_map/reduce_scatter | solution.py:70
  120.6 4.0 %bitcast_subtract_fusion = (f32[256,1024]{1,0:T(8,128)S(1)}, f32[256,1024]{1,0:T(8,128)S(1)}, f32[256,1024]{1,0:T(8,128)}, bf16[256,1024]{1,0:T(8,128)(2,1)}) fusion(f32[1,256,1024]{2,1,0:T(8,128)} %param.11, bf16[256,1024]{1,0:T(8,128)(2,1)} %reduce-scatter.2.cloned.1.call-done, f32[1,256,1024]{2,1,0:T(8,128)} %param.12, f32[1,256,1024]{2,1,0:T(8,128)} %param.13, ...), kind=kLoop, calls=%fused_computation.13 | loop fusion | flops 4194304 | bytes 7340036 | tf_op jit(solution)/shard_map/sub | solution.py:37
  124.6 0.0 all-gather.2.cloned.1.call-update
  125.3 74.6 %conditional.4 = (f32[256,1024]{1,0:T(8,128)}, f32[256,1024]{1,0:T(8,128)}, f32[256,1024]{1,0:T(8,128)}, f32[1]{0:T(128)}) conditional(s32[]{:T(128)} %clamp.3, (f32[256,1024]{1,0:T(8,128)S(1)}, f32[256,1024]{1,0:T(8,128)S(1)}, f32[256,1024]{1,0:T(8,128)}, f32[1]{0:T(128)}) %tuple.66, (f32[256,1024]{1,0:T(8,128)S(1)}, ...), branch_computations={%region_1.2_spmd, %region_2.3_spmd, %region_3.4_spmd, %region_4.5_... | conditional | flops 1572866 | bytes 15728852
  125.3 0.1 convert_element_type.130
  125.4 2.6 %collective-permute-start.8 = (bf16[256,1024]{1,0:T(8,128)(2,1)S(1)}, bf16[256,1024]{1,0:T(8,128)(2,1)S(1)}, u32[]{:S(2)}, u32[]{:S(2)}) collective-permute-start(bf16[256,1024]{1,0:T(8,128)(2,1)S(1)} %convert_element_type.130), channel_id=1, source_target_pairs={{192,0},{208,16},{224,32},{240,48},{0,64},{16,80},{32,96},{48,112}... | collective-permute-start | bytes 1572872 | tf_op jit(solution)/shard_map/cond/branch_2_fun/ppermute | solution.py:28
  128.0 0.1 convert_element_type.132
  128.1 2.9 %collective-permute-start.9 = (bf16[256,1024]{1,0:T(8,128)(2,1)S(1)}, bf16[256,1024]{1,0:T(8,128)(2,1)S(1)}, u32[]{:S(2)}, u32[]{:S(2)}) collective-permute-start(bf16[256,1024]{1,0:T(8,128)(2,1)S(1)} %convert_element_type.132), channel_id=1, source_target_pairs={{192,0},{208,16},{224,32},{240,48},{0,64},{16,80},{32,96},{48,112}... | collective-permute-start | bytes 1572872 | tf_op jit(solution)/shard_map/cond/branch_2_fun/ppermute | solution.py:28
  131.0 1.3 convert_element_type.134
  132.3 0.8 collective-permute-start.10
  133.8 60.4 %collective-permute-start.11 = (bf16[1]{0:T(256)(128)(2,1)}, bf16[1]{0:T(256)(128)(2,1)}, u32[]{:S(2)}, u32[]{:S(2)}) collective-permute-start(bf16[1]{0:T(256)(128)(2,1)} %convert_element_type.136), channel_id=1, source_target_pairs={{192,0},{208,16},{224,32},{240,48},{0,64},{16,80},{32,96},{48,112}... | collective-permute-start | bytes 14 | tf_op jit(solution)/shard_map/cond/branch_2_fun/ppermute | solution.py:28
  194.2 1.7 collective-permute-done.11
  196.5 0.0 collective-permute-done.8
  196.5 1.1 convert_element_type.162
  197.6 0.0 collective-permute-done.9
  197.6 1.1 convert_element_type.166
  198.7 0.0 collective-permute-done.10
  198.7 1.2 convert_element_type.170
  199.8 2.4 %multiply_bitcast_fusion.2 = f32[1,256,1024]{2,1,0:T(8,128)} fusion(f32[256,1024]{1,0:T(8,128)S(1)} %get-tuple-element.102, f32[256,1024]{1,0:T(8,128)} %get-tuple-element.98), kind=kLoop, calls=%fused_computation.17 | loop fusion | flops 524288 | bytes 3145728 | tf_op jit(solution)/shard_map/broadcast_in_dim | solution.py:88
  202.2 3.8 %multiply_bitcast_fusion = (f32[1,256,1024]{2,1,0:T(8,128)}, f32[1,256,1024]{2,1,0:T(8,128)}) fusion(f32[256,1024]{1,0:T(8,128)} %get-tuple-element.104, f32[256,1024]{1,0:T(8,128)} %get-tuple-element.100, f32[256,1024]{1,0:T(8,128)S(1)} %get-tuple-element.103, f32[256,1024]{1,0:T(8,128)} %get-tuple-element.99), kind=kLoop, calls=%fused_computation.15 | loop fusion | flops 1048576 | bytes 6291456 | tf_op jit(solution)/shard_map/broadcast_in_dim | solution.py:88
  206.0 0.0 all-gather.2.cloned.1.call-done
  206.0 9.1 %fusion.6 = bf16[1,512,1024]{1,2,0:T(8,128)(2,1)S(1)} fusion(bf16[4096,1024]{1,0:T(8,128)(2,1)} %all-gather.2.cloned.1.call-done, bf16[1,512,4096]{2,1,0:T(8,128)(2,1)} %param.15), kind=kOutput, calls=%fused_computation.5 | convolution fusion | flops 4295491584 | bytes 13631488 | tf_op jit(solution)/shard_map/dot_general | solution.py:63
  215.1 1.3 copy.12
Async XLA Ops:
  7.2 1.2 copy-start
  7.2 113.4 %reduce-scatter.2.cloned.1.call-start = ((), (), s32[]{:S(2)}) async-start(), calls=%async_computation.1 | async-start | bytes 8912896 | tf_op jit(solution)/shard_map/reduce_scatter | solution.py:70
  17.5 188.6 %all-gather.2.cloned.1.call-start = ((), (), s32[]{:S(2)}) async-start(), calls=%async_computation.2 | async-start | bytes 8912896 | tf_op jit(solution)/shard_map/all_gather | solution.py:65
  125.4 71.1 %collective-permute-start.8 = (bf16[256,1024]{1,0:T(8,128)(2,1)S(1)}, bf16[256,1024]{1,0:T(8,128)(2,1)S(1)}, u32[]{:S(2)}, u32[]{:S(2)}) collective-permute-start(bf16[256,1024]{1,0:T(8,128)(2,1)S(1)} %convert_element_type.130), channel_id=1, source_target_pairs={{192,0},{208,16},{224,32},{240,48},{0,64},{16,80},{32,96},{48,112}... | collective-permute-start | bytes 1572872 | tf_op jit(solution)/shard_map/cond/branch_2_fun/ppermute | solution.py:28
  128.1 69.5 %collective-permute-start.9 = (bf16[256,1024]{1,0:T(8,128)(2,1)S(1)}, bf16[256,1024]{1,0:T(8,128)(2,1)S(1)}, u32[]{:S(2)}, u32[]{:S(2)}) collective-permute-start(bf16[256,1024]{1,0:T(8,128)(2,1)S(1)} %convert_element_type.132), channel_id=1, source_target_pairs={{192,0},{208,16},{224,32},{240,48},{0,64},{16,80},{32,96},{48,112}... | collective-permute-start | bytes 1572872 | tf_op jit(solution)/shard_map/cond/branch_2_fun/ppermute | solution.py:28
  132.3 66.4 %collective-permute-start.10 = (bf16[256,1024]{1,0:T(8,128)(2,1)S(1)}, bf16[256,1024]{1,0:T(8,128)(2,1)S(1)}, u32[]{:S(2)}, u32[]{:S(2)}) collective-permute-start(bf16[256,1024]{1,0:T(8,128)(2,1)S(1)} %convert_element_type.134), channel_id=1, source_target_pairs={{192,0},{208,16},{224,32},{240,48},{0,64},{16,80},{32,96},{48,112}... | collective-permute-start | bytes 1572872 | tf_op jit(solution)/shard_map/cond/branch_2_fun/ppermute | solution.py:28
  133.8 62.1 %collective-permute-start.11 = (bf16[1]{0:T(256)(128)(2,1)}, bf16[1]{0:T(256)(128)(2,1)}, u32[]{:S(2)}, u32[]{:S(2)}) collective-permute-start(bf16[1]{0:T(256)(128)(2,1)} %convert_element_type.136), channel_id=1, source_target_pairs={{192,0},{208,16},{224,32},{240,48},{0,64},{16,80},{32,96},{48,112}... | collective-permute-start | bytes 14 | tf_op jit(solution)/shard_map/cond/branch_2_fun/ppermute | solution.py:28
Sparse Core Ops, SparseCore 0:
  17.6 102.9 reduce-scatter.1
  124.7 53.4 all-gather.1
where the time goes:
time: 225 us; the launch traced here: 224 us
  waiting for transfers between devices  104 us (46%)
  starting transfers between devices  66.9 us (30%)
  matrix products  18.2 us (8%)
  between operations  16.5 us (7%)
  other arithmetic  15 us (7%)
  local copies, waits for them, and re-layouts  2.49 us (1%)
    reduce_scatter x1, waiting for transfers between devices, per_device(): lax.psum_scatter(lax.dot_general(columns, cotangent_rows, (((0,), (0,)),...  102 us
    ppermute x4, starting transfers between devices, passed_along(): return lax.ppermute(block, axis, route)  66.8 us
    dot_general x1, matrix products, per_device(): jnp.dot(columns, lax.all_gather(weight, 'shard', axis=0, tiled=True), pre...  9.11 us
    dot_general x1, matrix products, per_device(): lax.dot_general(columns, cotangent_rows, (((0,), (0,)), ((), ())), prefer...  9.05 us
  transfers between devices with their start and end apart: 6, of which 2 were waited for; matrix products, arithmetic and copies ran while one was open for 5% of the time, Pallas kernels for 0%

commit v1 on v0

v1 whole, which is shorter than its diff:
```python
import functools

import jax
import jax.numpy as jnp
from jax import lax
from jax.experimental import pallas as pl
from jax.experimental.pallas import tpu as pltpu
from jax.sharding import PartitionSpec as P

STEP_COUNT = 20

beta_one = 0.9
beta_two = 0.999
rate = 0.003
epsilon = 1e-08

MESH = pl.DeviceIdType.MESH
REPLICAS = 16
ROWS = 256
FF = 1024
TOK = 512
QUARTERS = 4
QC = FF // QUARTERS
HALF = QC // 2
F32 = jnp.float32
BF16 = jnp.bfloat16

OPP, NXT, PRV, OWN = 0, 2, 4, 6


def adam(param, first, second):
    correct_one = 1.0 - beta_one ** (STEP_COUNT + 1)
    correct_two = 1.0 - beta_two ** (STEP_COUNT + 1)
    scaled = first * (rate / correct_one)
    return param - scaled / (jnp.sqrt(second * (1.0 / correct_two)) + epsilon)


def kernel(
    offset,
    p_hbm, m_hbm, v_hbm, pw_ref, tok_hbm, cot_hbm,
    np_hbm, nm_hbm, nv_hbm, nw_ref, act_hbm,
    tok_a, tok_b, cot, cot_t, par, mom, sec, par_b, par_r, weights,
    s1_out, s1_in, d_out, d_in, r_out, r_in, r_acc, own_acc, x_out, x_in,
    go_out, go_in, pw_out, pw_in, act_v,
    load_sem, tl_sem, ts_sem, tr_sem, cs_sem,
    wy_s, wy_r, wo_s, wo_r, wx_s, wx_r, wc_s, wc_r,
    s1_s, s1_r, d_s, d_r, r_s, r_r, x_s, x_r,
    gp_sem, gw_sem, go_s, go_r, st_sem, sa_sem,
):
    r = lax.axis_index("replica")
    s = lax.axis_index("shard")
    c = lax.rem(s, 2)
    x = lax.rem(lax.div(s, 2), 2)
    y = lax.div(s, 4)
    ys = [lax.rem(y + 2, 4), lax.rem(y + 1, 4), lax.rem(y + 3, 4), y]

    def at(yy, xx, cc):
        return (r, (yy * 2 + xx) * 2 + cc)

    up, down = at(ys[1], x, c), at(ys[2], x, c)
    across, sibling = at(y, 1 - x, c), at(y, x, 1 - c)
    ahead = (lax.rem(r + offset, REPLICAS), s)
    behind = (lax.rem(r + REPLICAS - offset, REPLICAS), s)

    def remote(src, dst, ss, rs, to):
        return pltpu.make_async_remote_copy(
            src_ref=src, dst_ref=dst, send_sem=ss, recv_sem=rs, device_id=to, device_id_type=MESH
        )

    def columns(i, core):
        block = ys[i // 2] * 2 + (x if i % 2 == 0 else 1 - x)
        return pl.ds(pl.multiple_of((block * 2 + core) * ROWS, ROWS), ROWS)

    def place(i):
        return pl.ds(i * ROWS, ROWS)

    loads = [
        pltpu.make_async_copy(p_hbm, par, load_sem.at[0]),
        pltpu.make_async_copy(cot_hbm, cot.at[0], load_sem.at[1]),
        pltpu.make_async_copy(m_hbm, mom, load_sem.at[2]),
        pltpu.make_async_copy(v_hbm, sec, load_sem.at[3]),
    ]
    load_a = [
        pltpu.make_async_copy(
            tok_hbm.at[:, columns(i, c)], tok_a.at[pl.ds(0, TOK), place(i)], tl_sem.at[i]
        )
        for i in range(8)
    ]
    load_b = [
        pltpu.make_async_copy(
            tok_hbm.at[:, columns(i, 1 - c)], tok_b.at[:, place(i)], tl_sem.at[8 + i]
        )
        for i in range(8)
    ]
    loads[0].start()
    loads[1].start()
    for copy in load_a:
        copy.start()

    barrier = pltpu.get_barrier_semaphore()
    for to in (up, down, across, sibling, ahead, behind):
        pl.semaphore_signal(barrier, inc=1, device_id=to, device_id_type=MESH)
    pl.semaphore_wait(barrier, 6)

    swap_cot = remote(cot_hbm, cot.at[1], cs_sem.at[0], cs_sem.at[1], sibling)
    swap_tok = [
        remote(
            tok_hbm.at[:, columns(i, 1 - c)],
            tok_a.at[pl.ds(TOK, TOK), place(i)],
            ts_sem.at[i], tr_sem.at[i], sibling,
        )
        for i in range(8)
    ]
    swap_cot.start()
    for copy in swap_tok:
        copy.start()

    def w(q, i, parity=0):
        return weights.at[q, parity, place(i), :]

    def w_half(q, i, h):
        return weights.at[q, 0, pl.ds(i * ROWS + h * HALF, HALF), :]

    def send_w_y(q):
        return [
            remote(w(q, OWN), w(q, PRV), wy_s.at[q, 0], wy_r.at[q, 0], up),
            remote(w(q, OWN), w(q, NXT), wy_s.at[q, 1], wy_r.at[q, 1], down),
        ]

    def send_w_opp(q):
        return [
            remote(w_half(q, PRV, 0), w_half(q, OPP, 0), wo_s.at[q, 0], wo_r.at[q, 0], up),
            remote(w_half(q, NXT, 1), w_half(q, OPP, 1), wo_s.at[q, 1], wo_r.at[q, 1], down),
        ]

    def send_w_x(q, i):
        g = i // 2
        return remote(w(q, i), w(q, i + 1), wx_s.at[q, g], wx_r.at[q, g], across)

    def send_w_core(q, i):
        return remote(w(q, i), w(q, i, 1), wc_s.at[q, i], wc_r.at[q, i], sibling)

    def send_s1(q):
        return [
            remote(s1_out.at[q, h], s1_in.at[q, h], s1_s.at[q, h], s1_r.at[q, h], to)
            for h, to in enumerate((up, down))
        ]

    def send_d(q):
        return [
            remote(d_out.at[q, h], d_in.at[q, h], d_s.at[q, h], d_r.at[q, h], to)
            for h, to in enumerate((up, down))
        ]

    def send_r(q):
        return [
            remote(r_out.at[q, h], r_in.at[q, h], r_s.at[q, h], r_r.at[q, h], to)
            for h, to in enumerate((up, down))
        ]

    def send_x(q):
        return remote(x_out.at[q], x_in.at[q], x_s.at[q], x_r.at[q], across)

    send_p = remote(par_b, par_r, gp_sem.at[0], gp_sem.at[1], ahead)
    send_pw = remote(pw_out, pw_in, gw_sem.at[0], gw_sem.at[1], ahead)

    def send_go(q):
        return remote(go_out.at[q], go_in.at[q], go_s.at[q], go_r.at[q], ahead)

    def quarter(q):
        return pl.ds(pl.multiple_of(q * QC, QC), QC)

    def stores(q):
        return [
            pltpu.make_async_copy(src.at[:, quarter(q)], dst.at[:, quarter(q)], st_sem.at[q, n])
            for n, (src, dst) in enumerate(((par, np_hbm), (mom, nm_hbm), (sec, nv_hbm)))
        ]

    def store_act(q):
        return pltpu.make_async_copy(act_v.at[q], act_hbm.at[:, quarter(q)], sa_sem.at[q])

    loads[0].wait()
    par_b[...] = par[...].astype(BF16)
    send_p.start()
    pw_out[...] = jnp.full(pw_out.shape, pw_ref[0], F32)
    send_pw.start()

    @pl.loop(0, QUARTERS)
    def _(q):
        weights[q, 0, place(OWN), :] = (par[:, quarter(q)] / pw_ref[0]).astype(BF16)

    loads[2].start()
    loads[3].start()
    for copy in load_b:
        copy.start()

    def tokens_ready(group):
        for i in (2 * group, 2 * group + 1):
            load_a[i].wait()
            swap_tok[i].wait_recv()

    def product(q, group):
        return jnp.dot(
            cot_t[q], tok_a[:, pl.ds(group * 2 * ROWS, 2 * ROWS)], preferred_element_type=F32
        )

    def issue(q):
        for copy in send_w_y(q):
            copy.start()
        send_w_x(q, OWN).start()
        send_w_core(q, OWN).start()

        @pl.when(q == 0)
        def _():
            loads[1].wait()
            swap_cot.wait_recv()
            tokens_ready(0)

        for n in range(2):
            cot_t[q, :, pl.ds(n * TOK, TOK)] = cot[n, :, quarter(q)].T
        far = product(q, 0)
        s1_out[q, 0] = far[:HALF].astype(BF16)
        s1_out[q, 1] = far[HALF:].astype(BF16)
        for copy in send_s1(q):
            copy.start()

        @pl.when(q == 0)
        def _():
            tokens_ready(1)

        after = product(q, 1)
        d_out[q, 0] = after[HALF:].astype(BF16)
        send_d(q)[0].start()
        r_acc[0] = after[:HALF]

        @pl.when(q == 0)
        def _():
            tokens_ready(2)

        before = product(q, 2)
        d_out[q, 1] = before[:HALF].astype(BF16)
        send_d(q)[1].start()
        r_acc[1] = before[HALF:]

        @pl.when(q == 0)
        def _():
            tokens_ready(3)

        own_acc[lax.rem(q, 2)] = product(q, 3)

    def forward_y(q):
        arrived, onward = send_w_y(q), send_w_opp(q)
        for n, i in ((0, PRV), (1, NXT)):
            arrived[n].wait_recv()
            onward[n].start()
            send_w_x(q, i).start()
            send_w_core(q, i).start()

    def relay(q):
        for n in range(2):
            send_s1(q)[n].wait_recv()
            r_out[q, n] = (r_acc[n] + s1_in[q, n].astype(F32)).astype(BF16)
            send_r(q)[n].start()

    def gather_sum(q):
        slot = lax.rem(q, 2)
        for n in range(2):
            send_d(q)[n].wait_recv()
            send_r(q)[n].wait_recv()
        top = own_acc[slot, :HALF] + r_in[q, 0].astype(F32) + d_in[q, 1].astype(F32)
        low = own_acc[slot, HALF:] + d_in[q, 0].astype(F32) + r_in[q, 1].astype(F32)
        x_out[q, :HALF] = top[:, ROWS:].astype(BF16)
        x_out[q, HALF:] = low[:, ROWS:].astype(BF16)
        send_x(q).start()
        own_acc[slot, :HALF, :ROWS] = top[:, :ROWS]
        own_acc[slot, HALF:, :ROWS] = low[:, :ROWS]

    def forward_opp(q):
        for copy in send_w_opp(q):
            copy.wait_recv()
        send_w_x(q, OPP).start()
        send_w_core(q, OPP).start()

    def update(q):
        @pl.when(q == 0)
        def _():
            loads[2].wait()
            loads[3].wait()

        send_x(q).wait_recv()
        gradient = (own_acc[lax.rem(q, 2), :, :ROWS] + x_in[q].astype(F32)).T
        first = beta_one * mom[:, quarter(q)] + (1.0 - beta_one) * gradient
        second = beta_two * sec[:, quarter(q)] + (1.0 - beta_two) * (gradient * gradient)
        go_out[q, 0] = first.astype(BF16)
        go_out[q, 1] = second.astype(BF16)
        send_go(q).start()
        mom[:, quarter(q)] = first
        sec[:, quarter(q)] = second
        par[:, quarter(q)] = adam(par[:, quarter(q)], first, second)

    def forward_x(q):
        for i in (OWN, PRV, NXT, OPP):
            send_w_x(q, i).wait_recv()
            send_w_core(q, i + 1).start()

    def activation(q):
        @pl.when(q == 0)
        def _():
            for copy in load_b:
                copy.wait()

        for i in range(8):
            send_w_core(q, i).wait_recv()

        @pl.loop(0, 2)
        def _(n):
            rows = pl.ds(pl.multiple_of(n * (TOK // 2), TOK // 2), TOK // 2)
            total = jnp.dot(tok_a[rows, :], weights[q, 0], preferred_element_type=F32)
            total += jnp.dot(tok_b[rows, :], weights[q, 1], preferred_element_type=F32)
            act_v[q, rows, :] = total.astype(BF16)

        store_act(q).start()

    def mix(q):
        @pl.when(q == 0)
        def _():
            send_p.wait_recv()

        send_go(q).wait_recv()
        first = go_in[q, 0].astype(F32)
        second = go_in[q, 1].astype(F32)
        stepped = adam(par_r[:, quarter(q)].astype(F32), first, second)
        par[:, quarter(q)] = 0.5 * (par[:, quarter(q)] + stepped)
        mom[:, quarter(q)] = 0.5 * (mom[:, quarter(q)] + first)
        sec[:, quarter(q)] = 0.5 * (sec[:, quarter(q)] + second)
        for copy in stores(q):
            copy.start()

    def step(t, _):
        @pl.when(jnp.logical_and(t >= 1, t <= 4))
        def _():
            forward_y(t - 1)
            relay(t - 1)

        @pl.when(t <= 3)
        def _():
            issue(t)

        @pl.when(jnp.logical_and(t >= 1, t <= 4))
        def _():
            gather_sum(t - 1)
            forward_opp(t - 1)
            update(t - 1)
            forward_x(t - 1)

        @pl.when(jnp.logical_and(t >= 2, t <= 5))
        def _():
            activation(t - 2)

        @pl.when(t >= 3)
        def _():
            mix(t - 3)

        return 0

    lax.fori_loop(0, 7, step, 0)

    send_pw.wait_recv()
    nw_ref[0] = 0.5 * (pw_ref[0] + pw_in[0, 0])

    swap_cot.wait_send()
    for copy in swap_tok:
        copy.wait_send()
    send_p.wait_send()
    send_pw.wait_send()

    @pl.loop(0, QUARTERS)
    def _(q):
        copies = send_w_y(q) + send_w_opp(q) + send_s1(q) + send_d(q) + send_r(q)
        copies += [send_w_x(q, i) for i in (OPP, NXT, PRV, OWN)]
        copies += [send_w_core(q, i) for i in range(8)]
        copies += [send_x(q), send_go(q)]
        for copy in copies:
            copy.wait_send()
        for copy in stores(q):
            copy.wait()
        store_act(q).wait()


def step_kernel(offset, collective_id):
    any_spec = pl.BlockSpec(memory_space=pl.ANY)
    smem = pl.BlockSpec(memory_space=pltpu.SMEM)
    Q = QUARTERS
    dma = pltpu.SemaphoreType.DMA
    scratch = [
        pltpu.VMEM((2 * TOK, 8 * ROWS), BF16),
        pltpu.VMEM((TOK, 8 * ROWS), BF16),
        pltpu.VMEM((2, TOK, FF), BF16),
        pltpu.VMEM((Q, QC, 2 * TOK), BF16),
        pltpu.VMEM((ROWS, FF), F32),
        pltpu.VMEM((ROWS, FF), F32),
        pltpu.VMEM((ROWS, FF), F32),
        pltpu.VMEM((ROWS, FF), BF16),
        pltpu.VMEM((ROWS, FF), BF16),
        pltpu.VMEM((Q, 2, 8 * ROWS, QC), BF16),
    ]
    scratch += [pltpu.VMEM((Q, 2, HALF, 2 * ROWS), BF16)] * 6
    scratch += [
        pltpu.VMEM((2, HALF, 2 * ROWS), F32),
        pltpu.VMEM((2, QC, 2 * ROWS), F32),
        pltpu.VMEM((Q, QC, ROWS), BF16),
        pltpu.VMEM((Q, QC, ROWS), BF16),
        pltpu.VMEM((Q, 2, ROWS, QC), BF16),
        pltpu.VMEM((Q, 2, ROWS, QC), BF16),
        pltpu.VMEM((8, 128), F32),
        pltpu.VMEM((8, 128), F32),
        pltpu.VMEM((Q, TOK, QC), BF16),
        dma((4,)), dma((16,)), dma((8,)), dma((8,)), dma((2,)),
        dma((Q, 2)), dma((Q, 2)), dma((Q, 2)), dma((Q, 2)),
        dma((Q, 4)), dma((Q, 4)), dma((Q, 8)), dma((Q, 8)),
        dma((Q, 2)), dma((Q, 2)), dma((Q, 2)), dma((Q, 2)), dma((Q, 2)), dma((Q, 2)),
        dma((Q,)), dma((Q,)),
        dma((2,)), dma((2,)), dma((Q,)), dma((Q,)), dma((Q, 3)), dma((Q,)),
    ]
    return pl.pallas_call(
        functools.partial(kernel, offset),
        out_shape=(
            jax.ShapeDtypeStruct((ROWS, FF), F32),
            jax.ShapeDtypeStruct((ROWS, FF), F32),
            jax.ShapeDtypeStruct((ROWS, FF), F32),
            jax.ShapeDtypeStruct((1,), F32),
            jax.ShapeDtypeStruct((TOK, FF), BF16),
        ),
        in_specs=[any_spec, any_spec, any_spec, smem, any_spec, any_spec],
        out_specs=(any_spec, any_spec, any_spec, smem, any_spec),
        scratch_shapes=scratch,
        compiler_params=pltpu.CompilerParams(
            collective_id=collective_id, has_side_effects=True, vmem_limit_bytes=56 << 20
        ),
        name=f"push_step_{offset}",
    )


def per_device(params, first_moment, second_moment, push_weight, tokens, cotangent, gossip_round):
    levels = REPLICAS.bit_length() - 1
    branches = [step_kernel(1 << level, level + 1) for level in range(levels)]
    new_params, new_first, new_second, new_weight, activation = lax.switch(
        gossip_round[0] % levels,
        branches,
        params[0], first_moment[0], second_moment[0], push_weight, tokens[0], cotangent[0],
    )
    return (new_params[None], new_first[None], new_second[None], new_weight, activation[None])


def solution(mesh):
    rows = P("replica", "shard", None)
    return jax.shard_map(
        per_device,
        mesh=mesh,
        in_specs=(rows, rows, rows, P("replica"), rows, rows, P()),
        out_specs=(rows, rows, rows, P("replica"), rows),
        check_vma=False,
    )
```

time: 225 us -> 130 us (0.58)
  the two profiles are of different devices: /device:TPU:32 before, /device:TPU:26 now
where the time goes in v1:
time: 130 us
  Pallas kernels  123 us (95%)
  local copies, waits for them, and re-layouts  3.88 us (3%)
  between operations  3 us (2%)
    pallas_call x1, Pallas kernels, per_device(): lax.switch(gossip_round[0] % levels, branches, params[0], first_moment[0]...  123 us
    unnamed x4, local copies, waits for them, and re-layouts  3.88 us

profile of v1, /device:TPU:26, one launch (start us, length us, event | category | flops | bytes accessed | tf_op | source)
XLA Modules:
  0.0 130.3 jit_solution(4131552068839333100)
XLA Ops:
  1.3 123.4 %conditional.1 = ((f32[256,1024]{1,0:T(8,128)S(1)}, f32[256,1024]{1,0:T(8,128)S(1)}, f32[256,1024]{1,0:T(8,128)S(1)}, f32[1]{0:T(128)}, bf16[512,1024]{1,0:T(8,128)(2,1)S(1)})) conditional(s32[]{:T(128)} %clamp.3, (f32[256,1024]{1,0:T(8,128)}, f32[256,1024]{1,0:T(8,128)}, f32[256,1024]{1,0:T(8,128)}, f32[1]{0:T(128)}, ...), branch_computations={%region_0.1_spmd, %region_1.2_spmd, %region_2.3_spmd, %region_3.4_... | conditional | bytes 8 | solution.py:447
  1.3 123.2 %push_step_1.1 = (f32[256,1024]{1,0:T(8,128)S(1)}, f32[256,1024]{1,0:T(8,128)S(1)}, f32[256,1024]{1,0:T(8,128)S(1)}, f32[1]{0:T(128)}, bf16[512,1024]{1,0:T(8,128)(2,1)S(1)}) custom-call(f32[256,1024]{1,0:T(8,128)} %get-tuple-element.78.p_hbm, f32[256,1024]{1,0:T(8,128)} %get-tuple-element.79.m_hbm, f32[256,1024]{1,0:T(8,128)} %get-tuple-element.80.v_hbm, ...), custom_call_target="tpu_custom_call" | custom-call | tf_op jit(solution)/shard_map/cond/branch_0_fun/push_step_1/pallas_call | solution.py:447
  124.7 1.0 copy.38
  125.7 1.0 copy.39
  126.7 1.0 copy.40
  128.2 1.0 copy.42

commit v2 on v1

v2 whole, which is shorter than its diff:
```python
import functools

import jax
import jax.numpy as jnp
from jax import lax
from jax.experimental import pallas as pl
from jax.experimental.pallas import tpu as pltpu
from jax.sharding import PartitionSpec as P

STEP_COUNT = 20

beta_one = 0.9
beta_two = 0.999
rate = 0.003
epsilon = 1e-08

MESH = pl.DeviceIdType.MESH
REPLICAS = 16
ROWS = 256
FF = 1024
TOK = 512
QUARTERS = 4
QC = FF // QUARTERS
HALF = QC // 2
F32 = jnp.float32
BF16 = jnp.bfloat16

OPP, NXT, PRV, OWN = 0, 2, 4, 6


ORDERS = {
    1: dict(
        activation=(15, 18, 17, 19),
        weights_y=(0, 11, 1, 10),
        issue_far=(8, 4, 3, 1),
        issue_own=(9, 4, 5, 2),
        mix=(19, 13, 16, 8),
        update=(13, 8, 11, 6),
        gather_sum=(9, 7, 8, 3),
        across_own=(12, 6, 9, 13),
        near_y_to_x=(9, -1, -1, -1),
        issue_near=(8, 4, 6, 2),
        across_far=(13, -1, -1, -1),
        far_y=(8, -1, -1, -1),
        near_z=(-1, 14, 13, 15),
        weights_x=(7, 2, 1, 5),
        relay=(8, 5, 7, 2),
        across_to_y=(-1, 8, 9, 13),
        across_near=(14, -1, -1, -1),
        far_both=(-1, 16, 15, 17),
        near_y=(7, 13, 11, 14),
    ),
    2: dict(
        issue_far=(7, 3, 12, 8),
        weights_y=(2, 11, 0, 15),
        gather_sum=(11, 8, 16, 13),
        weights_x=(0, 8, 2, 1),
        near_y=(9, 13, 2, 17),
        across_to_y=(-1, -1, -1, 15),
        across_far=(13, 16, 10, -1),
        far_y=(12, 15, 6, -1),
        across_near=(12, 15, 9, -1),
        across_own=(5, 11, 4, 12),
        near_y_to_x=(9, 13, 2, -1),
        issue_near=(8, 3, 13, 10),
        update=(12, 10, 18, 13),
        near_z=(-1, -1, -1, 18),
        far_both=(-1, -1, -1, 18),
        activation=(13, 16, 10, 18),
        mix=(13, 11, 18, 17),
        issue_own=(10, 5, 14, 8),
        relay=(8, 3, 13, 10),
    ),
    4: dict(
        activation=(19, 8, 17, 18),
        near_z=(-1, -1, -1, 16),
        across_to_y=(-1, -1, -1, 12),
        issue_own=(3, 4, 8, 9),
        far_both=(-1, -1, -1, 17),
        far_y=(17, 7, 13, -1),
        issue_near=(5, 2, 7, 10),
        gather_sum=(7, 5, 8, 12),
        across_far=(18, 7, 14, -1),
        relay=(6, 2, 7, 10),
        weights_x=(7, 0, 3, 1),
        across_near=(17, 7, 16, -1),
        near_y=(14, 4, 10, 15),
        across_own=(15, 2, 9, 7),
        weights_y=(11, 1, 7, 10),
        issue_far=(2, 1, 6, 7),
        update=(7, 6, 11, 13),
        near_y_to_x=(15, 5, 11, -1),
        mix=(12, 11, 16, 19),
        turn_back=(6, -1, -1, -1),
    ),
    8: dict(
        far_both=(-1, -1, -1, 14),
        near_z=(-1, -1, -1, 13),
        across_own=(5, 8, 4, 10),
        far_y=(5, 13, 10, -1),
        across_to_y=(-1, -1, -1, 12),
        weights_x=(0, 3, 1, 6),
        issue_near=(2, 9, 6, 5),
        relay=(2, 9, 7, 5),
        across_far=(7, 14, 11, -1),
        across_near=(7, 14, 10, -1),
        weights_y=(1, 10, 5, 12),
        issue_own=(3, 11, 8, 6),
        activation=(7, 15, 12, 14),
        issue_far=(1, 7, 4, 2),
        gather_sum=(3, 11, 8, 7),
        near_y=(1, 12, 7, 13),
        near_y_to_x=(1, 12, 7, -1),
        mix=(9, 16, 15, 12),
        update=(6, 12, 10, 7),
    ),
}


def adam(param, first, second):
    correct_one = 1.0 - beta_one ** (STEP_COUNT + 1)
    correct_two = 1.0 - beta_two ** (STEP_COUNT + 1)
    scaled = first * (rate / correct_one)
    return param - scaled / (jnp.sqrt(second * (1.0 / correct_two)) + epsilon)


def kernel(
    offset, order,
    p_hbm, m_hbm, v_hbm, pw_ref, tok_hbm, cot_hbm,
    par, mom, sec, nw_ref, act_hbm,
    tok_a, tok_b, cot, cot_t, par_b, par_r, par_relay, weights,
    s1_out, s1_in, d_out, d_in, r_out, r_in, r_acc, own_acc, x_out, x_in,
    go_out, go_in, pw_out, pw_in, act_v,
    load_sem, tl_sem, ts_sem, tr_sem, cs_sem,
    wy_s, wy_r, wo_s, wo_r, wz_s, wz_r, wq_s, wq_r, wx_s, wx_r, wc_s, wc_r,
    s1_s, s1_r, d_s, d_r, r_s, r_r, x_s, x_r,
    gp_sem, gw_sem, go_s, go_r, sa_sem,
):
    r = lax.axis_index("replica")
    s = lax.axis_index("shard")
    c = lax.rem(s, 2)
    x = lax.rem(lax.div(s, 2), 2)
    y = lax.div(s, 4)
    ys = [lax.rem(y + 2, 4), lax.rem(y + 1, 4), lax.rem(y + 3, 4), y]

    def at(yy, xx, cc):
        return (r, (yy * 2 + xx) * 2 + cc)

    up, down = at(ys[1], x, c), at(ys[2], x, c)
    across, sibling = at(y, 1 - x, c), at(y, x, 1 - c)
    ahead = (lax.rem(r + offset, REPLICAS), s)
    behind = (lax.rem(r + REPLICAS - offset, REPLICAS), s)

    def remote(src, dst, ss, rs, to):
        return pltpu.make_async_remote_copy(
            src_ref=src, dst_ref=dst, send_sem=ss, recv_sem=rs, device_id=to, device_id_type=MESH
        )

    def columns(i, core):
        block = ys[i // 2] * 2 + (x if i % 2 == 0 else 1 - x)
        return pl.ds(pl.multiple_of((block * 2 + core) * ROWS, ROWS), ROWS)

    def place(i):
        return pl.ds(i * ROWS, ROWS)

    loads = [
        pltpu.make_async_copy(p_hbm, par, load_sem.at[0]),
        pltpu.make_async_copy(cot_hbm, cot.at[0], load_sem.at[1]),
        pltpu.make_async_copy(m_hbm, mom, load_sem.at[2]),
        pltpu.make_async_copy(v_hbm, sec, load_sem.at[3]),
    ]
    load_a = [
        pltpu.make_async_copy(
            tok_hbm.at[:, columns(i, c)], tok_a.at[pl.ds(0, TOK), place(i)], tl_sem.at[i]
        )
        for i in range(8)
    ]
    load_b = [
        pltpu.make_async_copy(
            tok_hbm.at[:, columns(i, 1 - c)], tok_b.at[:, place(i)], tl_sem.at[8 + i]
        )
        for i in range(8)
    ]
    loads[0].start()
    loads[1].start()
    for copy in load_a:
        copy.start()

    barrier = pltpu.get_barrier_semaphore()
    partners = [up, down, across, sibling, ahead, behind]
    back = (lax.rem(r + REPLICAS - 6, REPLICAS), s)
    if offset == 4:
        partners += [back, (lax.rem(r + 6, REPLICAS), s)]
    for to in partners:
        pl.semaphore_signal(barrier, inc=1, device_id=to, device_id_type=MESH)
    pl.semaphore_wait(barrier, len(partners))

    def quarter(q):
        return pl.ds(pl.multiple_of(q * QC, QC), QC)

    def swap_cot(q):
        return remote(
            cot_hbm.at[:, quarter(q)], cot.at[1, :, quarter(q)],
            ts_sem.at[1], cs_sem.at[q], sibling,
        )

    swap_tok = [
        remote(
            tok_hbm.at[:, columns(i, 1 - c)],
            tok_a.at[pl.ds(TOK, TOK), place(i)],
            ts_sem.at[0], tr_sem.at[i], sibling,
        )
        for i in range(8)
    ]
    turns = sorted(range(QUARTERS), key=lambda q: order["issue_far"][q])
    swap_cot(turns[0]).start()
    for copy in swap_tok:
        copy.start()
    for q in turns[1:]:
        swap_cot(q).start()

    def w(q, i, parity=0):
        return weights.at[q, parity, place(i), :]

    def w_half(q, i, h):
        return weights.at[q, 0, pl.ds(i * ROWS + h * HALF, HALF), :]

    def send_w_y(q):
        return [
            remote(w(q, OWN), w(q, PRV), wy_s.at[0], wy_r.at[q, 0], up),
            remote(w(q, OWN), w(q, NXT), wy_s.at[0], wy_r.at[q, 1], down),
        ]

    def send_w_opp(q):
        return [
            remote(w_half(q, PRV, 0), w_half(q, OPP, 0), wo_s.at[0], wo_r.at[q, 0], up),
            remote(w_half(q, NXT, 1), w_half(q, OPP, 1), wo_s.at[0], wo_r.at[q, 1], down),
        ]

    def send_w_z(q):
        return [
            remote(w(q, OWN + 1), w(q, PRV + 1), wz_s.at[0], wz_r.at[q, 0], up),
            remote(w(q, OWN + 1), w(q, NXT + 1), wz_s.at[0], wz_r.at[q, 1], down),
        ]

    def send_w_far(q):
        return [
            remote(
                w_half(q, PRV + 1, 0), w_half(q, OPP + 1, 0), wq_s.at[0], wq_r.at[q, 0], up
            ),
            remote(
                w_half(q, NXT + 1, 1), w_half(q, OPP + 1, 1), wq_s.at[0], wq_r.at[q, 1], down
            ),
        ]

    def send_w_x(q, i):
        g = i // 2
        return remote(w(q, i), w(q, i + 1), wx_s.at[0], wx_r.at[q, g], across)

    def send_w_core(q, i):
        return remote(w(q, i), w(q, i, 1), wc_s.at[0], wc_r.at[q, i], sibling)

    def send_s1(q):
        return [
            remote(s1_out.at[q, h], s1_in.at[q, h], s1_s.at[0], s1_r.at[q, h], to)
            for h, to in enumerate((up, down))
        ]

    def send_d(q):
        return [
            remote(d_out.at[q, h], d_in.at[q, h], d_s.at[0], d_r.at[q, h], to)
            for h, to in enumerate((up, down))
        ]

    def send_r(q):
        return [
            remote(r_out.at[q, h], r_in.at[q, h], r_s.at[0], r_r.at[q, h], to)
            for h, to in enumerate((up, down))
        ]

    def send_x(q):
        return remote(x_out.at[q], x_in.at[q], x_s.at[0], x_r.at[q], across)

    two_ways = offset == 4
    near_half, far_half = pl.ds(0, ROWS // 2), pl.ds(ROWS // 2, ROWS // 2)
    if two_ways:
        send_p = remote(
            par_b.at[near_half], par_r.at[near_half], gp_sem.at[0], gp_sem.at[1], ahead
        )
        leg_one = remote(par_b.at[far_half], par_relay, gp_sem.at[2], gp_sem.at[3], back)
        leg_two = remote(par_relay, par_r.at[far_half], gp_sem.at[4], gp_sem.at[5], back)
    else:
        send_p = remote(par_b, par_r, gp_sem.at[0], gp_sem.at[1], ahead)
    send_pw = remote(pw_out, pw_in, gw_sem.at[0], gw_sem.at[1], ahead)

    def send_go(q):
        return remote(go_out.at[q], go_in.at[q], go_s.at[0], go_r.at[q], ahead)

    loads[0].wait()
    par_b[...] = par[...].astype(BF16)
    if two_ways:
        leg_one.start()
    send_p.start()
    pw_out[...] = jnp.full(pw_out.shape, pw_ref[0], F32)
    send_pw.start()

    @pl.loop(0, QUARTERS)
    def _(q):
        weights[q, 0, place(OWN), :] = (par[:, quarter(q)] / pw_ref[0]).astype(BF16)

    loads[2].start()
    loads[3].start()
    for copy in load_b:
        copy.start()

    def tokens_ready(group):
        for i in (2 * group, 2 * group + 1):
            load_a[i].wait()
            swap_tok[i].wait_recv()

    def product(q, group):
        return jnp.dot(
            cot_t[q], tok_a[:, pl.ds(group * 2 * ROWS, 2 * ROWS)], preferred_element_type=F32
        )

    def weights_y(q, first):
        for copy in send_w_y(q):
            copy.start()

    def weights_x(q, first):
        send_w_x(q, OWN).start()

    def issue_far(q, first):
        @pl.when(first)
        def _():
            loads[1].wait()
            tokens_ready(0)

        swap_cot(q).wait_recv()
        for n in range(2):
            cot_t[q, :, pl.ds(n * TOK, TOK)] = cot[n, :, quarter(q)].T
        far = product(q, 0)
        s1_out[q, 0] = far[:HALF].astype(BF16)
        s1_out[q, 1] = far[HALF:].astype(BF16)
        for copy in send_s1(q):
            copy.start()

    def issue_near(q, first):
        @pl.when(first)
        def _():
            tokens_ready(1)

        after = product(q, 1)
        d_out[q, 0] = after[HALF:].astype(BF16)
        send_d(q)[0].start()
        r_acc[q, 0] = after[:HALF]

        @pl.when(first)
        def _():
            tokens_ready(2)

        before = product(q, 2)
        d_out[q, 1] = before[:HALF].astype(BF16)
        send_d(q)[1].start()
        r_acc[q, 1] = before[HALF:]

    def issue_own(q, first):
        @pl.when(first)
        def _():
            tokens_ready(3)

        own_acc[q] = product(q, 3)

    def relay(q, first):
        for n in range(2):
            send_s1(q)[n].wait_recv()
            r_out[q, n] = (r_acc[q, n] + s1_in[q, n].astype(F32)).astype(BF16)
            send_r(q)[n].start()

    def gather_sum(q, first):
        for n in range(2):
            send_d(q)[n].wait_recv()
            send_r(q)[n].wait_recv()
        top = own_acc[q, :HALF] + r_in[q, 0].astype(F32) + d_in[q, 1].astype(F32)
        low = own_acc[q, HALF:] + d_in[q, 0].astype(F32) + r_in[q, 1].astype(F32)
        x_out[q, :HALF] = top[:, ROWS:].astype(BF16)
        x_out[q, HALF:] = low[:, ROWS:].astype(BF16)
        send_x(q).start()
        own_acc[q, :HALF, :ROWS] = top[:, :ROWS]
        own_acc[q, HALF:, :ROWS] = low[:, :ROWS]

    def update(q, first):
        @pl.when(first)
        def _():
            loads[2].wait()
            loads[3].wait()

        send_x(q).wait_recv()
        gradient = (own_acc[q, :, :ROWS] + x_in[q].astype(F32)).T
        fresh = beta_one * mom[:, quarter(q)] + (1.0 - beta_one) * gradient
        second = beta_two * sec[:, quarter(q)] + (1.0 - beta_two) * (gradient * gradient)
        go_out[q, 0] = fresh.astype(BF16)
        go_out[q, 1] = second.astype(BF16)
        send_go(q).start()
        mom[:, quarter(q)] = fresh
        sec[:, quarter(q)] = second
        par[:, quarter(q)] = adam(par[:, quarter(q)], fresh, second)

    def near_y(q, first):
        arrived, onward = send_w_y(q), send_w_opp(q)
        for n, i in ((0, PRV), (1, NXT)):
            arrived[n].wait_recv()
            onward[n].start()
            send_w_core(q, i).start()

    def near_y_to_x(q, first):
        send_w_x(q, PRV).start()
        send_w_x(q, NXT).start()

    def across_own(q, first):
        send_w_x(q, OWN).wait_recv()
        send_w_core(q, OWN + 1).start()

    def across_to_y(q, first):
        for copy in send_w_z(q):
            copy.start()

    def far_y(q, first):
        for copy in send_w_opp(q):
            copy.wait_recv()
        send_w_x(q, OPP).start()
        send_w_core(q, OPP).start()

    def across_near(q, first):
        for i in (PRV, NXT):
            send_w_x(q, i).wait_recv()
            send_w_core(q, i + 1).start()

    def across_far(q, first):
        send_w_x(q, OPP).wait_recv()
        send_w_core(q, OPP + 1).start()

    def near_z(q, first):
        arrived, onward = send_w_z(q), send_w_far(q)
        for n, i in ((0, PRV + 1), (1, NXT + 1)):
            arrived[n].wait_recv()
            onward[n].start()
            send_w_core(q, i).start()

    def far_both(q, first):
        for copy in send_w_opp(q):
            copy.wait_recv()
        send_w_core(q, OPP).start()
        for copy in send_w_far(q):
            copy.wait_recv()
        send_w_core(q, OPP + 1).start()

    def activation(q, first):
        @pl.when(first)
        def _():
            for copy in load_b:
                copy.wait()

        for i in range(8):
            send_w_core(q, i).wait_recv()

        @pl.loop(0, 2)
        def _(n):
            rows = pl.ds(pl.multiple_of(n * (TOK // 2), TOK // 2), TOK // 2)
            total = jnp.dot(tok_a[rows, :], weights[q, 0], preferred_element_type=F32)
            total += jnp.dot(tok_b[rows, :], weights[q, 1], preferred_element_type=F32)
            act_v[q, rows, :] = total.astype(BF16)

        store_act(q).start()

    def store_act(q):
        return pltpu.make_async_copy(act_v.at[q], act_hbm.at[:, quarter(q)], sa_sem.at[q])

    def turn_back(q, first):
        leg_one.wait_recv()
        leg_two.start()

    def mix(q, first):
        @pl.when(first)
        def _():
            send_p.wait_recv()
            if two_ways:
                leg_two.wait_recv()

        send_go(q).wait_recv()
        theirs = go_in[q, 0].astype(F32)
        second = go_in[q, 1].astype(F32)
        stepped = adam(par_r[:, quarter(q)].astype(F32), theirs, second)
        par[:, quarter(q)] = 0.5 * (par[:, quarter(q)] + stepped)
        mom[:, quarter(q)] = 0.5 * (mom[:, quarter(q)] + theirs)
        sec[:, quarter(q)] = 0.5 * (sec[:, quarter(q)] + second)

    events = {
        event.__name__: event
        for event in (
            weights_y, weights_x, issue_far, issue_near, issue_own, relay, gather_sum, update,
            near_y, near_y_to_x, across_own, across_to_y, far_y, across_near, across_far,
            near_z, far_both, activation, mix, turn_back,
        )
    }
    for n in turns:
        send_w_core(n, OWN).start()

    def run(i, _):
        for name, places in order.items():
            places = {q: n for q, n in enumerate(places) if n >= 0}
            here, q = False, 0
            for turn, n in places.items():
                here = jnp.logical_or(here, i == n)
                q = q + turn * (i == n).astype(jnp.int32)
            event = events[name]

            @pl.when(here)
            def _():
                event(q, i == min(places.values()))

        return 0

    passes = 1 + max(max(places) for places in order.values())
    lax.fori_loop(0, passes, run, 0)

    send_pw.wait_recv()
    nw_ref[0] = 0.5 * (pw_ref[0] + pw_in[0, 0])

    def sent(ref, sem):
        pltpu.make_async_copy(ref, ref, sem).wait()

    def finish():
        across = sum(4 if order["near_y_to_x"][q] >= 0 else 1 for q in range(QUARTERS))
        around = QUARTERS if "across_to_y" not in order else sum(
            n < 0 for n in order["across_to_y"]
        )
        around = QUARTERS - around
        sent(tok_a.at[pl.ds(TOK, TOK)], ts_sem.at[0])
        sent(cot.at[1], ts_sem.at[1])
        sent(weights.at[:, 0], wc_s.at[0])
        sent(weights.at[0, 0], wy_s.at[0])
        sent(weights.at[0, 0, pl.ds(0, 4 * ROWS)], wo_s.at[0])
        if around:
            sent(weights.at[0, 0, pl.ds(0, 2 * around * ROWS)], wz_s.at[0])
            sent(weights.at[0, 0, pl.ds(0, around * ROWS)], wq_s.at[0])
        sent(tok_b.at[pl.ds(0, across * (TOK // 16))], wx_s.at[0])
        sent(s1_out, s1_s.at[0])
        sent(d_out, d_s.at[0])
        sent(r_out, r_s.at[0])
        sent(x_out, x_s.at[0])
        sent(go_out, go_s.at[0])
        send_p.wait_send()
        send_pw.wait_send()
        for q in range(QUARTERS):
            store_act(q).wait()
        if two_ways:
            leg_one.wait_send()
            leg_two.wait_send()

    finish()


def leave_kernel(*refs):
    states, act, new_states, new_act, held, sems = refs[:3], refs[3], refs[4:7], refs[7], *refs[8:]
    blocks = [pl.ds(n * TOK // 4, TOK // 4) for n in range(4)]
    loads = [
        pltpu.make_async_copy(act.at[rows], held.at[rows], sems.at[n])
        for n, rows in enumerate(blocks)
    ]
    copies = [
        pltpu.make_async_copy(src, dst, sems.at[4 + n])
        for n, (src, dst) in enumerate(zip(states, new_states))
    ]
    stores = [
        pltpu.make_async_copy(held.at[rows], new_act.at[rows], sems.at[7 + n])
        for n, rows in enumerate(blocks)
    ]
    for copy in loads + copies:
        copy.start()
    for load, store in zip(loads, stores):
        load.wait()
        store.start()
    for copy in copies + stores:
        copy.wait()


def leave(states, activation):
    arrays = [pltpu.with_memory_space_constraint(a, pltpu.VMEM) for a in states] + [activation]
    return pl.pallas_call(
        leave_kernel,
        out_shape=tuple(jax.ShapeDtypeStruct(a.shape, a.dtype) for a in arrays),
        in_specs=[pl.BlockSpec(memory_space=pltpu.VMEM)] * len(states)
        + [pl.BlockSpec(memory_space=pl.ANY)],
        out_specs=tuple(pl.BlockSpec(memory_space=pl.ANY) for _ in arrays),
        scratch_shapes=[pltpu.VMEM((TOK, FF), BF16), pltpu.SemaphoreType.DMA((11,))],
        compiler_params=pltpu.CompilerParams(vmem_limit_bytes=8 << 20),
        name="leave",
    )(*arrays)


def step_kernel(offset, collective_id):
    any_spec = pl.BlockSpec(memory_space=pl.ANY)
    smem = pl.BlockSpec(memory_space=pltpu.SMEM)
    vmem = pl.BlockSpec(memory_space=pltpu.VMEM)
    Q = QUARTERS
    dma = pltpu.SemaphoreType.DMA
    scratch = [
        pltpu.VMEM((2 * TOK, 8 * ROWS), BF16),
        pltpu.VMEM((TOK, 8 * ROWS), BF16),
        pltpu.VMEM((2, TOK, FF), BF16),
        pltpu.VMEM((Q, QC, 2 * TOK), BF16),
        pltpu.VMEM((ROWS, FF), BF16),
        pltpu.VMEM((ROWS, FF), BF16),
        pltpu.VMEM((ROWS // 2, FF), BF16),
        pltpu.VMEM((Q, 2, 8 * ROWS, QC), BF16),
    ]
    scratch += [pltpu.VMEM((Q, 2, HALF, 2 * ROWS), BF16)] * 6
    scratch += [
        pltpu.VMEM((Q, 2, HALF, 2 * ROWS), F32),
        pltpu.VMEM((Q, QC, 2 * ROWS), F32),
        pltpu.VMEM((Q, QC, ROWS), BF16),
        pltpu.VMEM((Q, QC, ROWS), BF16),
        pltpu.VMEM((Q, 2, ROWS, QC), BF16),
        pltpu.VMEM((Q, 2, ROWS, QC), BF16),
        pltpu.VMEM((8, 128), F32),
        pltpu.VMEM((8, 128), F32),
        pltpu.VMEM((Q, TOK, QC), BF16),
        dma((4,)), dma((16,)), dma((2,)), dma((8,)), dma((Q,)),
        dma((1,)), dma((Q, 2)), dma((1,)), dma((Q, 2)),
        dma((1,)), dma((Q, 2)), dma((1,)), dma((Q, 2)),
        dma((1,)), dma((Q, 4)), dma((1,)), dma((Q, 8)),
        dma((1,)), dma((Q, 2)), dma((1,)), dma((Q, 2)), dma((1,)), dma((Q, 2)),
        dma((1,)), dma((Q,)),
        dma((6,)), dma((2,)), dma((1,)), dma((Q,)), dma((Q,)),
    ]
    return pl.pallas_call(
        functools.partial(kernel, offset, ORDERS[offset]),
        out_shape=(
            pltpu.VMEM((ROWS, FF), F32),
            pltpu.VMEM((ROWS, FF), F32),
            pltpu.VMEM((ROWS, FF), F32),
            jax.ShapeDtypeStruct((1,), F32),
            jax.ShapeDtypeStruct((TOK, FF), BF16),
        ),
        in_specs=[any_spec, any_spec, any_spec, smem, any_spec, any_spec],
        out_specs=(vmem, vmem, vmem, smem, any_spec),
        scratch_shapes=scratch,
        compiler_params=pltpu.CompilerParams(
            collective_id=collective_id, has_side_effects=True, vmem_limit_bytes=48 << 20
        ),
        name=f"push_step_{offset}",
    )


def per_device(params, first_moment, second_moment, push_weight, tokens, cotangent, gossip_round):
    levels = REPLICAS.bit_length() - 1
    branches = [step_kernel(1 << level, level + 1) for level in range(levels)]
    new_params, new_first, new_second, new_weight, activation = lax.switch(
        gossip_round[0] % levels,
        branches,
        params[0], first_moment[0], second_moment[0], push_weight, tokens[0], cotangent[0],
    )
    new_params, new_first, new_second, activation = leave(
        (new_params, new_first, new_second), activation
    )
    return (new_params[None], new_first[None], new_second[None], new_weight, activation[None])


def solution(mesh):
    rows = P("replica", "shard", None)
    return jax.shard_map(
        per_device,
        mesh=mesh,
        in_specs=(rows, rows, rows, P("replica"), rows, rows, P()),
        out_specs=(rows, rows, rows, P("replica"), rows),
        check_vma=False,
    )
```

time: 130 us -> 94.2 us (0.72)
  the two profiles are of different devices: /device:TPU:26 before, /device:TPU:4 now
where the time goes in v2:
time: 94.2 us; the launch traced here: 94 us
  Pallas kernels  90.7 us (96%)
  between operations  3.07 us (3%)
    pallas_call x1, Pallas kernels, per_device(): lax.switch(gossip_round[0] % levels, branches, params[0], first_moment[0]...  88 us
    pallas_call x1, Pallas kernels, leave(): pl.pallas_call(leave_kernel, out_shape=tuple((jax.ShapeDtypeStruct(a.shap...  2.72 us

profile of v2, /device:TPU:4, one launch (start us, length us, event | category | flops | bytes accessed | tf_op | source)
XLA Modules:
  0.0 94.0 jit_solution(12632066858571039859)
XLA Ops:
  1.3 88.2 %conditional.1 = ((f32[256,1024]{1,0:T(8,128)S(1)}, f32[256,1024]{1,0:T(8,128)S(1)}, f32[256,1024]{1,0:T(8,128)S(1)}, f32[1]{0:T(128)}, bf16[512,1024]{1,0:T(8,128)(2,1)})) conditional(s32[]{:T(128)} %clamp.3, (f32[256,1024]{1,0:T(8,128)}, f32[256,1024]{1,0:T(8,128)}, f32[256,1024]{1,0:T(8,128)}, f32[1]{0:T(128)}, ...), branch_computations={%region_0.1_spmd, %region_1.2_spmd, %region_2.3_spmd, %region_3.4_... | conditional | bytes 8 | solution.py:659
  1.3 88.0 %push_step_1.1 = (f32[256,1024]{1,0:T(8,128)S(1)}, f32[256,1024]{1,0:T(8,128)S(1)}, f32[256,1024]{1,0:T(8,128)S(1)}, f32[1]{0:T(128)}, bf16[512,1024]{1,0:T(8,128)(2,1)}) custom-call(f32[256,1024]{1,0:T(8,128)} %get-tuple-element.48.p_hbm, f32[256,1024]{1,0:T(8,128)} %get-tuple-element.49.m_hbm, f32[256,1024]{1,0:T(8,128)} %get-tuple-element.50.v_hbm, ...), custom_call_target="tpu_custom_call" | custom-call | tf_op jit(solution)/shard_map/cond/branch_0_fun/push_step_1/pallas_call | solution.py:659
  89.5 2.7 %leave.1 = (f32[256,1024]{1,0:T(8,128)}, f32[256,1024]{1,0:T(8,128)}, f32[256,1024]{1,0:T(8,128)}, bf16[512,1024]{1,0:T(8,128)(2,1)}) custom-call(f32[256,1024]{1,0:T(8,128)S(1)} %get-tuple-element.86.refs_0_, f32[256,1024]{1,0:T(8,128)S(1)} %get-tuple-element.87.refs_1_, f32[256,1024]{1,0:T(8,128)S(1)} %get-tuple-element.88.refs_2_, ...), custom_call_target="tpu_custom_call" | custom-call | tf_op jit(solution)/shard_map/leave/pallas_call | solution.py:590

commit v3 on v2

--- a/solution.py
+++ b/solution.py
@@ -30,89 +30,95 @@
 
 ORDERS = {
     1: dict(
-        activation=(15, 18, 17, 19),
-        weights_y=(0, 11, 1, 10),
-        issue_far=(8, 4, 3, 1),
-        issue_own=(9, 4, 5, 2),
-        mix=(19, 13, 16, 8),
-        update=(13, 8, 11, 6),
-        gather_sum=(9, 7, 8, 3),
-        across_own=(12, 6, 9, 13),
-        near_y_to_x=(9, -1, -1, -1),
-        issue_near=(8, 4, 6, 2),
-        across_far=(13, -1, -1, -1),
-        far_y=(8, -1, -1, -1),
-        near_z=(-1, 14, 13, 15),
-        weights_x=(7, 2, 1, 5),
-        relay=(8, 5, 7, 2),
-        across_to_y=(-1, 8, 9, 13),
-        across_near=(14, -1, -1, -1),
-        far_both=(-1, 16, 15, 17),
-        near_y=(7, 13, 11, 14),
+        across_far=(24, -1, -1, -1),
+        across_own=(21, 3, 7, 12),
+        weights_y=(2, 13, 12, 20),
+        gather_sum=(15, 8, 10, 14),
+        issue_far=(8, 2, 4, 7),
+        params_x=(5, 3, 9, 6),
+        weights_x=(20, 1, 0, 2),
+        near_y_to_x=(20, -1, -1, -1),
+        across_to_y=(-1, 15, 13, 16),
+        update=(17, 10, 11, 16),
+        near_z=(-1, 19, 20, 21),
+        activation_most=(24, 20, 22, 23),
+        across_near=(23, -1, -1, -1),
+        activation_rest=(25, 21, 23, 24),
+        far_y=(20, -1, -1, -1),
+        pass_on=(20, 13, 14, 18),
+        issue_near=(11, 2, 5, 10),
+        relay=(11, 4, 6, 10),
+        issue_own=(8, 3, 6, 9),
+        mix=(25, 17, 18, 21),
+        near_y=(11, 19, 20, 21),
+        far_both=(-1, 20, 22, 23),
     ),
     2: dict(
-        issue_far=(7, 3, 12, 8),
-        weights_y=(2, 11, 0, 15),
-        gather_sum=(11, 8, 16, 13),
-        weights_x=(0, 8, 2, 1),
-        near_y=(9, 13, 2, 17),
-        across_to_y=(-1, -1, -1, 15),
-        across_far=(13, 16, 10, -1),
-        far_y=(12, 15, 6, -1),
-        across_near=(12, 15, 9, -1),
-        across_own=(5, 11, 4, 12),
-        near_y_to_x=(9, 13, 2, -1),
-        issue_near=(8, 3, 13, 10),
-        update=(12, 10, 18, 13),
-        near_z=(-1, -1, -1, 18),
-        far_both=(-1, -1, -1, 18),
-        activation=(13, 16, 10, 18),
-        mix=(13, 11, 18, 17),
-        issue_own=(10, 5, 14, 8),
-        relay=(8, 3, 13, 10),
+        activation_most=(11, 20, 13, 21),
+        across_near=(10, 19, 9, -1),
+        far_y=(5, 19, 10, -1),
+        near_z=(-1, -1, -1, 20),
+        relay=(10, 15, 4, 12),
+        near_y=(3, 16, 4, 19),
+        near_y_to_x=(3, 16, 4, -1),
+        issue_far=(5, 13, 3, 7),
+        across_far=(10, 20, 13, -1),
+        gather_sum=(13, 17, 8, 14),
+        weights_x=(1, 10, 2, 14),
+        issue_near=(9, 14, 3, 10),
+        activation_rest=(12, 20, 13, 21),
+        issue_own=(8, 13, 3, 7),
+        update=(13, 19, 11, 15),
+        weights_y=(0, 13, 2, 16),
+        mix=(18, 21, 13, 17),
+        far_both=(-1, -1, -1, 20),
+        across_own=(5, 15, 6, 18),
+        across_to_y=(-1, -1, -1, 18),
     ),
     4: dict(
-        activation=(19, 8, 17, 18),
-        near_z=(-1, -1, -1, 16),
-        across_to_y=(-1, -1, -1, 12),
-        issue_own=(3, 4, 8, 9),
+        issue_near=(6, 2, 10, 5),
+        issue_own=(6, 2, 9, 4),
+        weights_x=(1, 0, 2, 3),
+        relay=(7, 2, 10, 5),
         far_both=(-1, -1, -1, 17),
-        far_y=(17, 7, 13, -1),
-        issue_near=(5, 2, 7, 10),
-        gather_sum=(7, 5, 8, 12),
-        across_far=(18, 7, 14, -1),
-        relay=(6, 2, 7, 10),
-        weights_x=(7, 0, 3, 1),
+        weights_y=(12, 0, 9, 11),
+        across_to_y=(-1, -1, -1, 14),
         across_near=(17, 7, 16, -1),
-        near_y=(14, 4, 10, 15),
-        across_own=(15, 2, 9, 7),
-        weights_y=(11, 1, 7, 10),
-        issue_far=(2, 1, 6, 7),
-        update=(7, 6, 11, 13),
-        near_y_to_x=(15, 5, 11, -1),
-        mix=(12, 11, 16, 19),
-        turn_back=(6, -1, -1, -1),
+        far_y=(16, 7, 15, -1),
+        near_y=(15, 3, 10, 14),
+        issue_far=(5, 1, 8, 2),
+        near_y_to_x=(15, 5, 10, -1),
+        update=(11, 5, 14, 7),
+        across_far=(19, 9, 16, -1),
+        activation_most=(19, 8, 17, 16),
+        across_own=(12, 2, 10, 6),
+        near_z=(-1, -1, -1, 15),
+        turn_back=(5, -1, -1, -1),
+        gather_sum=(9, 3, 13, 6),
+        activation_rest=(19, 9, 17, 18),
+        mix=(15, 12, 19, 13),
     ),
     8: dict(
-        far_both=(-1, -1, -1, 14),
-        near_z=(-1, -1, -1, 13),
-        across_own=(5, 8, 4, 10),
-        far_y=(5, 13, 10, -1),
-        across_to_y=(-1, -1, -1, 12),
-        weights_x=(0, 3, 1, 6),
-        issue_near=(2, 9, 6, 5),
-        relay=(2, 9, 7, 5),
-        across_far=(7, 14, 11, -1),
-        across_near=(7, 14, 10, -1),
-        weights_y=(1, 10, 5, 12),
-        issue_own=(3, 11, 8, 6),
-        activation=(7, 15, 12, 14),
-        issue_far=(1, 7, 4, 2),
-        gather_sum=(3, 11, 8, 7),
-        near_y=(1, 12, 7, 13),
-        near_y_to_x=(1, 12, 7, -1),
-        mix=(9, 16, 15, 12),
-        update=(6, 12, 10, 7),
+        activation_rest=(8, 18, 16, 17),
+        issue_own=(10, 4, 2, 8),
+        near_y_to_x=(3, 15, 10, -1),
+        far_both=(-1, -1, -1, 16),
+        across_own=(6, 8, 9, 3),
+        issue_near=(8, 3, 1, 5),
+        weights_x=(1, 6, 7, 0),
+        gather_sum=(11, 6, 3, 9),
+        across_far=(6, 17, 14, -1),
+        far_y=(5, 16, 13, -1),
+        across_near=(6, 16, 12, -1),
+        across_to_y=(-1, -1, -1, 13),
+        activation_most=(7, 17, 13, 16),
+        relay=(10, 3, 2, 6),
+        update=(13, 9, 5, 10),
+        mix=(18, 13, 10, 16),
+        weights_y=(0, 10, 6, 11),
+        issue_far=(7, 2, 0, 4),
+        near_y=(2, 14, 9, 15),
+        near_z=(-1, -1, -1, 15),
     ),
 }
 
@@ -127,14 +133,14 @@
 def kernel(
     offset, order,
     p_hbm, m_hbm, v_hbm, pw_ref, tok_hbm, cot_hbm,
-    par, mom, sec, nw_ref, act_hbm,
+    par, mom, sec, nw_hbm, act_hbm,
     tok_a, tok_b, cot, cot_t, par_b, par_r, par_relay, weights,
     s1_out, s1_in, d_out, d_in, r_out, r_in, r_acc, own_acc, x_out, x_in,
-    go_out, go_in, pw_out, pw_in, act_v,
+    go_out, go_in, go_relay, pw_out, pw_in, nw_ref, act_acc, act_v,
     load_sem, tl_sem, ts_sem, tr_sem, cs_sem,
     wy_s, wy_r, wo_s, wo_r, wz_s, wz_r, wq_s, wq_r, wx_s, wx_r, wc_s, wc_r,
     s1_s, s1_r, d_s, d_r, r_s, r_r, x_s, x_r,
-    gp_sem, gw_sem, go_s, go_r, sa_sem,
+    gp_sem, gw_sem, go_s, go_r, gl_s, gl_r, gq_s, gq_r, sa_sem, nw_sem,
 ):
     r = lax.axis_index("replica")
     s = lax.axis_index("shard")
@@ -148,8 +154,10 @@
 
     up, down = at(ys[1], x, c), at(ys[2], x, c)
     across, sibling = at(y, 1 - x, c), at(y, x, 1 - c)
-    ahead = (lax.rem(r + offset, REPLICAS), s)
-    behind = (lax.rem(r + REPLICAS - offset, REPLICAS), s)
+    two_legs = offset == 1
+    peer = s if not two_legs else at(y, 1 - x, c)[1]
+    ahead = (lax.rem(r + offset, REPLICAS), peer)
+    behind = (lax.rem(r + REPLICAS - offset, REPLICAS), peer)
 
     def remote(src, dst, ss, rs, to):
         return pltpu.make_async_remote_copy(
@@ -171,13 +179,13 @@
     ]
     load_a = [
         pltpu.make_async_copy(
-            tok_hbm.at[:, columns(i, c)], tok_a.at[pl.ds(0, TOK), place(i)], tl_sem.at[i]
+            tok_hbm.at[:, columns(i, c)], tok_a.at[pl.ds(0, TOK), place(i)], tl_sem.at[i // 2]
         )
         for i in range(8)
     ]
     load_b = [
         pltpu.make_async_copy(
-            tok_hbm.at[:, columns(i, 1 - c)], tok_b.at[:, place(i)], tl_sem.at[8 + i]
+            tok_hbm.at[:, columns(i, 1 - c)], tok_b.at[:, place(i)], tl_sem.at[4]
         )
         for i in range(8)
     ]
@@ -208,7 +216,7 @@
         remote(
             tok_hbm.at[:, columns(i, 1 - c)],
             tok_a.at[pl.ds(TOK, TOK), place(i)],
-            ts_sem.at[0], tr_sem.at[i], sibling,
+            ts_sem.at[0], tr_sem.at[i // 2], sibling,
         )
         for i in range(8)
     ]
@@ -227,29 +235,29 @@
 
     def send_w_y(q):
         return [
-            remote(w(q, OWN), w(q, PRV), wy_s.at[0], wy_r.at[q, 0], up),
-            remote(w(q, OWN), w(q, NXT), wy_s.at[0], wy_r.at[q, 1], down),
+            remote(w(q, OWN), w(q, PRV), wy_s.at[0], wy_r.at[q], up),
+            remote(w(q, OWN), w(q, NXT), wy_s.at[0], wy_r.at[q], down),
         ]
 
     def send_w_opp(q):
         return [
-            remote(w_half(q, PRV, 0), w_half(q, OPP, 0), wo_s.at[0], wo_r.at[q, 0], up),
-            remote(w_half(q, NXT, 1), w_half(q, OPP, 1), wo_s.at[0], wo_r.at[q, 1], down),
+            remote(w_half(q, PRV, 0), w_half(q, OPP, 0), wo_s.at[0], wo_r.at[q], up),
+            remote(w_half(q, NXT, 1), w_half(q, OPP, 1), wo_s.at[0], wo_r.at[q], down),
         ]
 
     def send_w_z(q):
         return [
-            remote(w(q, OWN + 1), w(q, PRV + 1), wz_s.at[0], wz_r.at[q, 0], up),
-            remote(w(q, OWN + 1), w(q, NXT + 1), wz_s.at[0], wz_r.at[q, 1], down),
+            remote(w(q, OWN + 1), w(q, PRV + 1), wz_s.at[0], wz_r.at[q], up),
+            remote(w(q, OWN + 1), w(q, NXT + 1), wz_s.at[0], wz_r.at[q], down),
         ]
 
     def send_w_far(q):
         return [
             remote(
-                w_half(q, PRV + 1, 0), w_half(q, OPP + 1, 0), wq_s.at[0], wq_r.at[q, 0], up
+                w_half(q, PRV + 1, 0), w_half(q, OPP + 1, 0), wq_s.at[0], wq_r.at[q], up
             ),
             remote(
-                w_half(q, NXT + 1, 1), w_half(q, OPP + 1, 1), wq_s.at[0], wq_r.at[q, 1], down
+                w_half(q, NXT + 1, 1), w_half(q, OPP + 1, 1), wq_s.at[0], wq_r.at[q], down
             ),
         ]
 
@@ -258,23 +266,23 @@
         return remote(w(q, i), w(q, i + 1), wx_s.at[0], wx_r.at[q, g], across)
 
     def send_w_core(q, i):
-        return remote(w(q, i), w(q, i, 1), wc_s.at[0], wc_r.at[q, i], sibling)
+        return remote(w(q, i), w(q, i, 1), wc_s.at[0], wc_r.at[q, min(i // 2, 1)], sibling)
 
     def send_s1(q):
         return [
-            remote(s1_out.at[q, h], s1_in.at[q, h], s1_s.at[0], s1_r.at[q, h], to)
+            remote(s1_out.at[q, h], s1_in.at[q, h], s1_s.at[0], s1_r.at[q], to)
             for h, to in enumerate((up, down))
         ]
 
     def send_d(q):
         return [
-            remote(d_out.at[q, h], d_in.at[q, h], d_s.at[0], d_r.at[q, h], to)
+            remote(d_out.at[q, h], d_in.at[q, h], d_s.at[0], d_r.at[q], to)
             for h, to in enumerate((up, down))
         ]
 
     def send_r(q):
         return [
-            remote(r_out.at[q, h], r_in.at[q, h], r_s.at[0], r_r.at[q, h], to)
+            remote(r_out.at[q, h], r_in.at[q, h], r_s.at[0], r_r.at[q], to)
             for h, to in enumerate((up, down))
         ]
 
@@ -294,13 +302,27 @@
     send_pw = remote(pw_out, pw_in, gw_sem.at[0], gw_sem.at[1], ahead)
 
     def send_go(q):
-        return remote(go_out.at[q], go_in.at[q], go_s.at[0], go_r.at[q], ahead)
+        source = go_relay if two_legs else go_out
+        return remote(source.at[q], go_in.at[q], go_s.at[0], go_r.at[q], ahead)
+
+    states = pl.ds(0, 2)
+
+    def leg_states(q):
+        return remote(
+            go_out.at[q], go_relay.at[q, states], gl_s.at[0], gl_r.at[q], across
+        )
+
+    def leg_params(q):
+        return remote(
+            par_b.at[:, quarter(q)], go_relay.at[q, 2], gq_s.at[0], gq_r.at[q], across
+        )
 
     loads[0].wait()
     par_b[...] = par[...].astype(BF16)
     if two_ways:
         leg_one.start()
-    send_p.start()
+    if not two_legs:
+        send_p.start()
     pw_out[...] = jnp.full(pw_out.shape, pw_ref[0], F32)
     send_pw.start()
 
@@ -313,10 +335,13 @@
     for copy in load_b:
         copy.start()
 
+    def ended(ref, sem):
+        pltpu.make_async_copy(ref, ref, sem).wait()
+
     def tokens_ready(group):
-        for i in (2 * group, 2 * group + 1):
-            load_a[i].wait()
-            swap_tok[i].wait_recv()
+        pair = pl.ds(group * 2 * ROWS, 2 * ROWS)
+        ended(tok_a.at[pl.ds(0, TOK), pair], tl_sem.at[group])
+        ended(tok_a.at[pl.ds(TOK, TOK), pair], tr_sem.at[group])
 
     def product(q, group):
         return jnp.dot(
@@ -372,15 +397,14 @@
         own_acc[q] = product(q, 3)
 
     def relay(q, first):
+        ended(s1_in.at[q], s1_r.at[q])
         for n in range(2):
-            send_s1(q)[n].wait_recv()
             r_out[q, n] = (r_acc[q, n] + s1_in[q, n].astype(F32)).astype(BF16)
             send_r(q)[n].start()
 
     def gather_sum(q, first):
-        for n in range(2):
-            send_d(q)[n].wait_recv()
-            send_r(q)[n].wait_recv()
+        ended(d_in.at[q], d_r.at[q])
+        ended(r_in.at[q], r_r.at[q])
         top = own_acc[q, :HALF] + r_in[q, 0].astype(F32) + d_in[q, 1].astype(F32)
         low = own_acc[q, HALF:] + d_in[q, 0].astype(F32) + r_in[q, 1].astype(F32)
         x_out[q, :HALF] = top[:, ROWS:].astype(BF16)
@@ -401,15 +425,15 @@
         second = beta_two * sec[:, quarter(q)] + (1.0 - beta_two) * (gradient * gradient)
         go_out[q, 0] = fresh.astype(BF16)
         go_out[q, 1] = second.astype(BF16)
-        send_go(q).start()
+        (leg_states if two_legs else send_go)(q).start()
         mom[:, quarter(q)] = fresh
         sec[:, quarter(q)] = second
         par[:, quarter(q)] = adam(par[:, quarter(q)], fresh, second)
 
     def near_y(q, first):
-        arrived, onward = send_w_y(q), send_w_opp(q)
+        ended(weights.at[q, 0, pl.ds(NXT * ROWS, 2 * ROWS)], wy_r.at[q])
+        onward = send_w_opp(q)
         for n, i in ((0, PRV), (1, NXT)):
-            arrived[n].wait_recv()
             onward[n].start()
             send_w_core(q, i).start()
 
@@ -426,8 +450,7 @@
             copy.start()
 
     def far_y(q, first):
-        for copy in send_w_opp(q):
-            copy.wait_recv()
+        ended(w(q, OPP), wo_r.at[q])
         send_w_x(q, OPP).start()
         send_w_core(q, OPP).start()
 
@@ -441,40 +464,64 @@
         send_w_core(q, OPP + 1).start()
 
     def near_z(q, first):
-        arrived, onward = send_w_z(q), send_w_far(q)
+        ended(weights.at[q, 0, pl.ds(NXT * ROWS, 2 * ROWS)], wz_r.at[q])
+        onward = send_w_far(q)
         for n, i in ((0, PRV + 1), (1, NXT + 1)):
-            arrived[n].wait_recv()
             onward[n].start()
             send_w_core(q, i).start()
 
     def far_both(q, first):
-        for copy in send_w_opp(q):
-            copy.wait_recv()
+        ended(w(q, OPP), wo_r.at[q])
         send_w_core(q, OPP).start()
-        for copy in send_w_far(q):
-            copy.wait_recv()
+        ended(w(q, OPP + 1), wq_r.at[q])
         send_w_core(q, OPP + 1).start()
 
-    def activation(q, first):
+    def activation_part(q, slots, rows):
+        total = jnp.dot(tok_a[rows, slots], weights[q, 0, slots], preferred_element_type=F32)
+        return total + jnp.dot(
+            tok_b[rows, slots], weights[q, 1, slots], preferred_element_type=F32
+        )
+
+    def halves(body):
+        @pl.loop(0, 2)
+        def _(n):
+            body(pl.ds(pl.multiple_of(n * (TOK // 2), TOK // 2), TOK // 2))
+
+    last, others = pl.ds(0, 2 * ROWS), pl.ds(2 * ROWS, 6 * ROWS)
+
+    def activation_most(q, first):
         @pl.when(first)
         def _():
-            for copy in load_b:
-                copy.wait()
-
-        for i in range(8):
-            send_w_core(q, i).wait_recv()
-
-        @pl.loop(0, 2)
-        def _(n):
-            rows = pl.ds(pl.multiple_of(n * (TOK // 2), TOK // 2), TOK // 2)
-            total = jnp.dot(tok_a[rows, :], weights[q, 0], preferred_element_type=F32)
-            total += jnp.dot(tok_b[rows, :], weights[q, 1], preferred_element_type=F32)
-            act_v[q, rows, :] = total.astype(BF16)
+            ended(tok_b, tl_sem.at[4])
+
+        ended(weights.at[q, 1, others], wc_r.at[q, 1])
+
+        @halves
+        def _(rows):
+            act_acc[q, rows] = activation_part(q, others, rows)
+
+    def activation_rest(q, first):
+        ended(weights.at[q, 1, last], wc_r.at[q, 0])
+
+        @halves
+        def _(rows):
+            total = act_acc[q, rows] + activation_part(q, last, rows)
+            act_v[q, rows] = total.astype(BF16)
 
         store_act(q).start()
+
+    store_nw = pltpu.make_async_copy(nw_ref, nw_hbm, nw_sem.at[0])
 
     def store_act(q):
         return pltpu.make_async_copy(act_v.at[q], act_hbm.at[:, quarter(q)], sa_sem.at[q])
+
+    def params_x(q, first):
+        leg_params(q).start()
+
+    def pass_on(q, first):
+        leg_params(q).wait_recv()
+        leg_states(q).wait_recv()
+        send_go(q).start()
 
     def turn_back(q, first):
         leg_one.wait_recv()
@@ -483,14 +530,19 @@
     def mix(q, first):
         @pl.when(first)
         def _():
-            send_p.wait_recv()
+            if not two_legs:
+                send_p.wait_recv()
             if two_ways:
                 leg_two.wait_recv()
+            send_pw.wait_recv()
+            nw_ref[0] = 0.5 * (pw_ref[0] + pw_in[0, 0])
+            store_nw.start()
 
         send_go(q).wait_recv()
         theirs = go_in[q, 0].astype(F32)
         second = go_in[q, 1].astype(F32)
-        stepped = adam(par_r[:, quarter(q)].astype(F32), theirs, second)
+        param = go_in[q, 2] if two_legs else par_r[:, quarter(q)]
+        stepped = adam(param.astype(F32), theirs, second)
         par[:, quarter(q)] = 0.5 * (par[:, quarter(q)] + stepped)
         mom[:, quarter(q)] = 0.5 * (mom[:, quarter(q)] + theirs)
         sec[:, quarter(q)] = 0.5 * (sec[:, quarter(q)] + second)
@@ -500,7 +552,8 @@
         for event in (
             weights_y, weights_x, issue_far, issue_near, issue_own, relay, gather_sum, update,
             near_y, near_y_to_x, across_own, across_to_y, far_y, across_near, across_far,
-            near_z, far_both, activation, mix, turn_back,
+            near_z, far_both, activation_most, activation_rest, mix, turn_back,
+            params_x, pass_on,
         )
     }
     for n in turns:
@@ -524,36 +577,33 @@
     passes = 1 + max(max(places) for places in order.values())
     lax.fori_loop(0, passes, run, 0)
 
-    send_pw.wait_recv()
-    nw_ref[0] = 0.5 * (pw_ref[0] + pw_in[0, 0])
-
-    def sent(ref, sem):
-        pltpu.make_async_copy(ref, ref, sem).wait()
-
     def finish():
-        across = sum(4 if order["near_y_to_x"][q] >= 0 else 1 for q in range(QUARTERS))
-        around = QUARTERS if "across_to_y" not in order else sum(
-            n < 0 for n in order["across_to_y"]
-        )
-        around = QUARTERS - around
-        sent(tok_a.at[pl.ds(TOK, TOK)], ts_sem.at[0])
-        sent(cot.at[1], ts_sem.at[1])
-        sent(weights.at[:, 0], wc_s.at[0])
-        sent(weights.at[0, 0], wy_s.at[0])
-        sent(weights.at[0, 0, pl.ds(0, 4 * ROWS)], wo_s.at[0])
+        around = sum(n >= 0 for n in order.get("across_to_y", ()))
+        across = QUARTERS + 3 * (QUARTERS - around)
+        ended(tok_a.at[pl.ds(TOK, TOK)], ts_sem.at[0])
+        ended(cot.at[1], ts_sem.at[1])
+        ended(weights.at[:, 0], wc_s.at[0])
+        ended(weights.at[0, 0], wy_s.at[0])
+        ended(weights.at[0, 0, pl.ds(0, 4 * ROWS)], wo_s.at[0])
         if around:
-            sent(weights.at[0, 0, pl.ds(0, 2 * around * ROWS)], wz_s.at[0])
-            sent(weights.at[0, 0, pl.ds(0, around * ROWS)], wq_s.at[0])
-        sent(tok_b.at[pl.ds(0, across * (TOK // 16))], wx_s.at[0])
-        sent(s1_out, s1_s.at[0])
-        sent(d_out, d_s.at[0])
-        sent(r_out, r_s.at[0])
-        sent(x_out, x_s.at[0])
-        sent(go_out, go_s.at[0])
-        send_p.wait_send()
+            ended(weights.at[0, 0, pl.ds(0, 2 * around * ROWS)], wz_s.at[0])
+            ended(weights.at[0, 0, pl.ds(0, around * ROWS)], wq_s.at[0])
+        ended(tok_b.at[pl.ds(0, across * (TOK // 16))], wx_s.at[0])
+        ended(s1_out, s1_s.at[0])
+        ended(d_out, d_s.at[0])
+        ended(r_out, r_s.at[0])
+        ended(x_out, x_s.at[0])
+        if two_legs:
+            ended(go_out, gl_s.at[0])
+            ended(par_b, gq_s.at[0])
+            ended(go_relay, go_s.at[0])
+        else:
+            ended(go_out, go_s.at[0])
+            send_p.wait_send()
         send_pw.wait_send()
         for q in range(QUARTERS):
             store_act(q).wait()
+        store_nw.wait()
         if two_ways:
             leg_one.wait_send()
             leg_two.wait_send()
@@ -568,12 +618,14 @@
         pltpu.make_async_copy(act.at[rows], held.at[rows], sems.at[n])
         for n, rows in enumerate(blocks)
     ]
+    parts = [pl.ds(n * ROWS // 2, ROWS // 2) for n in range(2)]
     copies = [
-        pltpu.make_async_copy(src, dst, sems.at[4 + n])
+        pltpu.make_async_copy(src.at[rows], dst.at[rows], sems.at[8 + 2 * n + k])
         for n, (src, dst) in enumerate(zip(states, new_states))
+        for k, rows in enumerate(parts)
     ]
     stores = [
-        pltpu.make_async_copy(held.at[rows], new_act.at[rows], sems.at[7 + n])
+        pltpu.make_async_copy(held.at[rows], new_act.at[rows], sems.at[4 + n])
         for n, rows in enumerate(blocks)
     ]
     for copy in loads + copies:
@@ -593,7 +645,7 @@
         in_specs=[pl.BlockSpec(memory_space=pltpu.VMEM)] * len(states)
         + [pl.BlockSpec(memory_space=pl.ANY)],
         out_specs=tuple(pl.BlockSpec(memory_space=pl.ANY) for _ in arrays),
-        scratch_shapes=[pltpu.VMEM((TOK, FF), BF16), pltpu.SemaphoreType.DMA((11,))],
+        scratch_shapes=[pltpu.VMEM((TOK, FF), BF16), pltpu.SemaphoreType.DMA((14,))],
         compiler_params=pltpu.CompilerParams(vmem_limit_bytes=8 << 20),
         name="leave",
     )(*arrays)
@@ -622,17 +674,21 @@
         pltpu.VMEM((Q, QC, ROWS), BF16),
         pltpu.VMEM((Q, QC, ROWS), BF16),
         pltpu.VMEM((Q, 2, ROWS, QC), BF16),
-        pltpu.VMEM((Q, 2, ROWS, QC), BF16),
+        pltpu.VMEM((Q, 3 if offset == 1 else 2, ROWS, QC), BF16),
+        pltpu.VMEM((Q, 3, ROWS, QC) if offset == 1 else (16, 128), BF16),
         pltpu.VMEM((8, 128), F32),
         pltpu.VMEM((8, 128), F32),
+        pltpu.SMEM((1,), F32),
+        pltpu.VMEM((Q, TOK, QC), F32),
         pltpu.VMEM((Q, TOK, QC), BF16),
-        dma((4,)), dma((16,)), dma((2,)), dma((8,)), dma((Q,)),
-        dma((1,)), dma((Q, 2)), dma((1,)), dma((Q, 2)),
-        dma((1,)), dma((Q, 2)), dma((1,)), dma((Q, 2)),
-        dma((1,)), dma((Q, 4)), dma((1,)), dma((Q, 8)),
-        dma((1,)), dma((Q, 2)), dma((1,)), dma((Q, 2)), dma((1,)), dma((Q, 2)),
+        dma((4,)), dma((5,)), dma((2,)), dma((4,)), dma((Q,)),
+        dma((1,)), dma((Q,)), dma((1,)), dma((Q,)),
+        dma((1,)), dma((Q,)), dma((1,)), dma((Q,)),
+        dma((1,)), dma((Q, 4)), dma((1,)), dma((Q, 2)),
+        dma((1,)), dma((Q,)), dma((1,)), dma((Q,)), dma((1,)), dma((Q,)),
         dma((1,)), dma((Q,)),
-        dma((6,)), dma((2,)), dma((1,)), dma((Q,)), dma((Q,)),
+        dma((6,)), dma((2,)), dma((1,)), dma((Q,)), dma((1,)), dma((Q,)), dma((1,)), dma((Q,)),
+        dma((Q,)), dma((1,)),
     ]
     return pl.pallas_call(
         functools.partial(kernel, offset, ORDERS[offset]),
@@ -644,7 +700,7 @@
             jax.ShapeDtypeStruct((TOK, FF), BF16),
         ),
         in_specs=[any_spec, any_spec, any_spec, smem, any_spec, any_spec],
-        out_specs=(vmem, vmem, vmem, smem, any_spec),
+        out_specs=(vmem, vmem, vmem, any_spec, any_spec),
         scratch_shapes=scratch,
         compiler_params=pltpu.CompilerParams(
             collective_id=collective_id, has_side_effects=True, vmem_limit_bytes=48 << 20

time: 94.2 us -> 84.6 us (0.90)
  the two profiles are of different devices: /device:TPU:4 before, /device:TPU:1 now
where the time goes in v3:
time: 84.6 us; the launch traced here: 84.4 us
  Pallas kernels  80.9 us (96%)
  between operations  3.07 us (4%)
    pallas_call x1, Pallas kernels, per_device(): lax.switch(gossip_round[0] % levels, branches, params[0], first_moment[0]...  78.2 us
    pallas_call x1, Pallas kernels, leave(): pl.pallas_call(leave_kernel, out_shape=tuple((jax.ShapeDtypeStruct(a.shap...  2.75 us

profile of v3, /device:TPU:1, one launch (start us, length us, event | category | flops | bytes accessed | tf_op | source)
XLA Modules:
  0.0 84.4 jit_solution(12520700992534384473)
XLA Ops:
  1.3 78.6 %conditional.1 = ((f32[256,1024]{1,0:T(8,128)S(1)}, f32[256,1024]{1,0:T(8,128)S(1)}, f32[256,1024]{1,0:T(8,128)S(1)}, f32[1]{0:T(128)}, bf16[512,1024]{1,0:T(8,128)(2,1)})) conditional(s32[]{:T(128)} %clamp.3, (f32[256,1024]{1,0:T(8,128)}, f32[256,1024]{1,0:T(8,128)}, f32[256,1024]{1,0:T(8,128)}, f32[1]{0:T(128)}, ...), branch_computations={%region_0.1_spmd, %region_1.2_spmd, %region_2.3_spmd, %region_3.4_... | conditional | bytes 8 | solution.py:715
  1.3 78.2 %push_step_4.1 = (f32[256,1024]{1,0:T(8,128)S(1)}, f32[256,1024]{1,0:T(8,128)S(1)}, f32[256,1024]{1,0:T(8,128)S(1)}, f32[1]{0:T(128)}, bf16[512,1024]{1,0:T(8,128)(2,1)}) custom-call(f32[256,1024]{1,0:T(8,128)} %get-tuple-element.60.p_hbm, f32[256,1024]{1,0:T(8,128)} %get-tuple-element.61.m_hbm, f32[256,1024]{1,0:T(8,128)} %get-tuple-element.62.v_hbm, ...), custom_call_target="tpu_custom_call" | custom-call | tf_op jit(solution)/shard_map/cond/branch_2_fun/push_step_4/pallas_call | solution.py:715
  79.9 2.7 %leave.1 = (f32[256,1024]{1,0:T(8,128)}, f32[256,1024]{1,0:T(8,128)}, f32[256,1024]{1,0:T(8,128)}, bf16[512,1024]{1,0:T(8,128)(2,1)}) custom-call(f32[256,1024]{1,0:T(8,128)S(1)} %get-tuple-element.86.refs_0_, f32[256,1024]{1,0:T(8,128)S(1)} %get-tuple-element.87.refs_1_, f32[256,1024]{1,0:T(8,128)S(1)} %get-tuple-element.88.refs_2_, ...), custom_call_target="tpu_custom_call" | custom-call | tf_op jit(solution)/shard_map/leave/pallas_call | solution.py:642

commit v4 on v3

--- a/solution.py
+++ b/solution.py
@@ -99,26 +99,26 @@
         mix=(15, 12, 19, 13),
     ),
     8: dict(
-        activation_rest=(8, 18, 16, 17),
-        issue_own=(10, 4, 2, 8),
-        near_y_to_x=(3, 15, 10, -1),
-        far_both=(-1, -1, -1, 16),
-        across_own=(6, 8, 9, 3),
-        issue_near=(8, 3, 1, 5),
-        weights_x=(1, 6, 7, 0),
-        gather_sum=(11, 6, 3, 9),
-        across_far=(6, 17, 14, -1),
-        far_y=(5, 16, 13, -1),
-        across_near=(6, 16, 12, -1),
-        across_to_y=(-1, -1, -1, 13),
-        activation_most=(7, 17, 13, 16),
-        relay=(10, 3, 2, 6),
-        update=(13, 9, 5, 10),
-        mix=(18, 13, 10, 16),
-        weights_y=(0, 10, 6, 11),
-        issue_far=(7, 2, 0, 4),
-        near_y=(2, 14, 9, 15),
-        near_z=(-1, -1, -1, 15),
+        across_own=(12, 4, 9, 15),
+        weights_y=(11, 0, 1, 15),
+        across_to_y=(-1, -1, -1, 15),
+        far_y=(16, 4, 11, -1),
+        activation_rest=(18, 6, 15, 19),
+        issue_own=(11, 5, 4, 9),
+        weights_x=(1, 3, 2, 7),
+        update=(17, 10, 6, 13),
+        issue_far=(9, 4, 3, 6),
+        gather_sum=(15, 7, 4, 10),
+        across_far=(17, 5, 14, -1),
+        near_z=(-1, -1, -1, 17),
+        near_y=(14, 2, 8, 17),
+        activation_most=(16, 5, 13, 18),
+        across_near=(15, 4, 12, -1),
+        near_y_to_x=(14, 3, 8, -1),
+        issue_near=(12, 4, 3, 7),
+        relay=(13, 5, 3, 7),
+        far_both=(-1, -1, -1, 18),
+        mix=(19, 15, 12, 18),
     ),
 }
 
@@ -562,15 +562,13 @@
     def run(i, _):
         for name, places in order.items():
             places = {q: n for q, n in enumerate(places) if n >= 0}
-            here, q = False, 0
-            for turn, n in places.items():
-                here = jnp.logical_or(here, i == n)
-                q = q + turn * (i == n).astype(jnp.int32)
+            here = functools.reduce(jnp.logical_or, [i == n for n in places.values()])
             event = events[name]
 
             @pl.when(here)
             def _():
-                event(q, i == min(places.values()))
+                turns_here = [turn * (i == n).astype(jnp.int32) for turn, n in places.items()]
+                event(functools.reduce(jnp.add, turns_here), i == min(places.values()))
 
         return 0
 
@@ -713,7 +711,7 @@
     levels = REPLICAS.bit_length() - 1
     branches = [step_kernel(1 << level, level + 1) for level in range(levels)]
     new_params, new_first, new_second, new_weight, activation = lax.switch(
-        gossip_round[0] % levels,
+        gossip_round[0] & (levels - 1),
         branches,
         params[0], first_moment[0], second_moment[0], push_weight, tokens[0], cotangent[0],
     )

time: 84.6 us -> 89.8 us (1.061)
  the two profiles are of different devices: /device:TPU:1 before, /device:TPU:26 now
where the time goes in v4:
time: 89.8 us; the launch traced here: 89.5 us
  Pallas kernels  86.1 us (96%)
  between operations  3.06 us (3%)
    pallas_call x1, Pallas kernels, per_device(): lax.switch(gossip_round[0] & levels - 1, branches, params[0], first_momen...  83.3 us
    pallas_call x1, Pallas kernels, leave(): pl.pallas_call(leave_kernel, out_shape=tuple((jax.ShapeDtypeStruct(a.shap...  2.75 us

profile of v4, /device:TPU:26, one launch (start us, length us, event | category | flops | bytes accessed | tf_op | source)
XLA Modules:
  0.0 89.5 jit_solution(3989950815522773263)
XLA Ops:
  1.3 83.7 %conditional.1 = ((f32[256,1024]{1,0:T(8,128)S(1)}, f32[256,1024]{1,0:T(8,128)S(1)}, f32[256,1024]{1,0:T(8,128)S(1)}, f32[1]{0:T(128)}, bf16[512,1024]{1,0:T(8,128)(2,1)})) conditional(s32[]{:T(128)} %bitcast, (f32[256,1024]{1,0:T(8,128)}, f32[256,1024]{1,0:T(8,128)}, f32[256,1024]{1,0:T(8,128)}, f32[1]{0:T(128)}, ...), branch_computations={%region_0.0_spmd, %region_1.0_spmd, %region_2.0_spmd, %region_3.0_... | conditional | bytes 8 | solution.py:713
  1.5 83.3 %push_step_8.1 = (f32[256,1024]{1,0:T(8,128)S(1)}, f32[256,1024]{1,0:T(8,128)S(1)}, f32[256,1024]{1,0:T(8,128)S(1)}, f32[1]{0:T(128)}, bf16[512,1024]{1,0:T(8,128)(2,1)}) custom-call(f32[256,1024]{1,0:T(8,128)} %get-tuple-element.66.p_hbm, f32[256,1024]{1,0:T(8,128)} %get-tuple-element.67.m_hbm, f32[256,1024]{1,0:T(8,128)} %get-tuple-element.68.v_hbm, ...), custom_call_target="tpu_custom_call" | custom-call | tf_op jit(solution)/shard_map/cond/branch_3_fun/push_step_8/pallas_call | solution.py:713
  85.0 2.7 %leave.1 = (f32[256,1024]{1,0:T(8,128)}, f32[256,1024]{1,0:T(8,128)}, f32[256,1024]{1,0:T(8,128)}, bf16[512,1024]{1,0:T(8,128)(2,1)}) custom-call(f32[256,1024]{1,0:T(8,128)S(1)} %get-tuple-element.86.refs_0_, f32[256,1024]{1,0:T(8,128)S(1)} %get-tuple-element.87.refs_1_, f32[256,1024]{1,0:T(8,128)S(1)} %get-tuple-element.88.refs_2_, ...), custom_call_target="tpu_custom_call" | custom-call | tf_op jit(solution)/shard_map/leave/pallas_call | solution.py:640
